TPU v7x, 32 devices: a whole 2x2x4 slice. The times are simulated.
32 devices in a mesh: seq: 8 (over z, y), mp: 4 (over x, core).
Axes of the slice: x: 2, y: 2, z: 4, core: 2. Of those that a mesh axis runs over, the one named last changes fastest.
Arguments:
- query_states: bfloat16 [1024, 2048], P('seq', 'mp'), may hold values from -6 to 6
- key_states: bfloat16 [1024, 2048], P('seq', 'mp'), may hold values from -6 to 6
- value_states: bfloat16 [1024, 2048], P('seq', 'mp'), may hold values from -6 to 6
- lengths: int32 [8], replicated, may hold values from 32 to 128
- tokens: int32 [1024, 4], P('seq'), may hold values from 0 to 1023
- assignment: int32 [1024], P('seq'), may hold values from 0 to 2047, as said below
- proj_weight: bfloat16 [2048, 1024], P(('mp', 'seq')), may hold values from -0.5 to 0.5
- query_weight: bfloat16 [1024, 512], P('seq'), may hold values from -0.1875 to 0.1875
- key_weight: bfloat16 [1024, 512], P('seq'), may hold values from -0.1875 to 0.1875
- value_weight: bfloat16 [1024, 512], P('seq'), may hold values from -0.1875 to 0.1875
- out_weight: bfloat16 [512, 1024], P('seq'), may hold values from -0.25 to 0.25
- logit_weight: bfloat16 [1024, 1024], P('seq'), may hold values from -0.5 to 0.5
- embedding: bfloat16 [1024, 1024], P('seq'), may hold values from -6 to 6
- gain_attn: float32 [1024], replicated, may hold values from 0.1 to 1.9
- gain_head: float32 [1024], replicated, may hold values from 0.1 to 1.9
Outputs:
- context: bfloat16 [1024, 2048], P('seq', 'mp')
- context_grad: bfloat16 [1024, 2048], P('seq', 'mp')
- slot_loss: float32 [2048], P(('seq', 'mp'))
Inputs may be any that keep to these rules, and one draw needn't show every extreme that they name: `assignment`: the frame with index f, on seq device s = f // 128, takes slot d * 256 + s * 32 + k for some depth group d and some 0 <= k < 32; no two frames share a slot.
All inputs are finite; a program needn't handle non-finite values.
Results may differ from a plain program's by a relative error of at most 0.028.
Values may be sent and summed in bfloat16 or wider, within the bound.
A program may use at most 64 MiB of HBM per device.

v0:
```python
import math

import jax
import jax.numpy as jnp
from jax import lax
from jax.sharding import PartitionSpec as P

HEAD_D = 64
HEAD_T = 128
CB = 4


NORM_EPS = 1e-05


def for_sending(value):

    def short(part):
        return part.astype(jnp.bfloat16) if part.dtype == jnp.float32 else part

    return jax.tree.map(short, value)


def rms_scale(inputs, gain):
    return inputs * lax.rsqrt(jnp.mean(inputs * inputs, axis=-1, keepdims=True) + NORM_EPS) * gain


def depth_losses(
    hidden,
    token_ids,
    live_mask,
    query_weight,
    key_weight,
    value_weight,
    out_weight,
    logit_weight,
    embedding,
    gain_attn,
    gain_head,
):
    frame_count = hidden.shape[0]
    model_width = hidden.shape[1]
    head_count = query_weight.shape[1] // HEAD_D
    row_count = frame_count * CB
    looked = jnp.take(embedding, token_ids[:, : CB - 1], axis=0).astype(jnp.float32)
    looked = jnp.concatenate(
        [jnp.zeros((frame_count, 1, model_width), jnp.float32), looked], axis=1
    )
    inputs = hidden.astype(jnp.float32)[:, None, :] + looked
    normed = rms_scale(inputs, gain_attn).astype(jnp.bfloat16).reshape(row_count, model_width)
    head_shape = (frame_count, CB, head_count, HEAD_D)
    query_rows = (
        jnp.dot(normed, query_weight, preferred_element_type=jnp.float32)
        .astype(jnp.bfloat16)
        .reshape(head_shape)
    )
    key_rows = (
        jnp.dot(normed, key_weight, preferred_element_type=jnp.float32)
        .astype(jnp.bfloat16)
        .reshape(head_shape)
    )
    value_rows = (
        jnp.dot(normed, value_weight, preferred_element_type=jnp.float32)
        .astype(jnp.bfloat16)
        .reshape(head_shape)
    )
    scores = jnp.einsum(
        "fqhd,fkhd->fhqk", query_rows, key_rows, preferred_element_type=jnp.float32
    ) / math.sqrt(HEAD_D)
    places = jnp.arange(CB)
    causal = (places[None, :] <= places[:, None]).astype(jnp.float32)
    weights = jnp.exp(scores) * causal
    totals = jnp.sum(weights, axis=-1)
    mixture = jnp.einsum(
        "fhqk,fkhd->fqhd",
        weights.astype(jnp.bfloat16),
        value_rows,
        preferred_element_type=jnp.float32,
    )
    mixture = mixture / jnp.transpose(totals, (0, 2, 1))[..., None]
    mixture = mixture.astype(jnp.bfloat16).reshape(row_count, head_count * HEAD_D)
    residual = inputs.reshape(row_count, model_width) + jnp.dot(
        mixture, out_weight, preferred_element_type=jnp.float32
    )
    head_in = rms_scale(residual, gain_head).astype(jnp.bfloat16)
    logits = jnp.dot(head_in, logit_weight, preferred_element_type=jnp.float32)
    log_total = jnp.log(jnp.sum(jnp.exp(logits), axis=-1))
    target = jnp.take_along_axis(logits, token_ids.reshape(row_count, 1), axis=1)[:, 0]
    per_frame = jnp.sum((log_total - target).reshape(frame_count, CB), axis=1)
    return per_frame * live_mask


def body(
    query_states,
    key_states,
    value_states,
    lengths,
    tokens,
    assignment,
    proj_weight,
    query_weight,
    key_weight,
    value_weight,
    out_weight,
    logit_weight,
    embedding,
    gain_attn,
    gain_head,
):
    seq_count = lax.axis_size("seq")
    seq_index = lax.axis_index("seq")
    frame_count = query_states.shape[0]
    local_width = query_states.shape[1]
    head_count = local_width // HEAD_T
    length = lengths[seq_index]
    places = jnp.arange(frame_count)
    visible = (places[None, :] <= places[:, None]).astype(jnp.float32)
    key_shape = (frame_count, head_count, HEAD_T)
    scores = jnp.einsum(
        "qhd,khd->hqk",
        query_states.reshape(key_shape),
        key_states.reshape(key_shape),
        preferred_element_type=jnp.float32,
    ) / math.sqrt(HEAD_T)
    weights = jnp.exp(scores) * visible[None, :, :]
    totals = jnp.sum(weights, axis=-1)
    mixture = jnp.einsum(
        "hqk,khd->qhd",
        weights.astype(jnp.bfloat16),
        value_states.reshape(key_shape),
        preferred_element_type=jnp.float32,
    )
    mixture = mixture / jnp.transpose(totals)[:, :, None]
    live_mask = (places < length).astype(jnp.float32)
    context = (mixture.reshape(frame_count, local_width) * live_mask[:, None]).astype(jnp.bfloat16)
    gathered = (
        lax.all_gather(query_weight, "seq", axis=0, tiled=True),
        lax.all_gather(key_weight, "seq", axis=0, tiled=True),
        lax.all_gather(value_weight, "seq", axis=0, tiled=True),
        lax.all_gather(out_weight, "seq", axis=0, tiled=True),
        lax.all_gather(logit_weight, "seq", axis=0, tiled=True),
        lax.all_gather(embedding, "seq", axis=0, tiled=True),
        lax.all_gather(proj_weight, "seq", axis=0, tiled=True),
    )
    query_full, key_full, value_full, out_full, logit_full, embed_full, proj_quarter = gathered
    slot_cap = 2 * frame_count
    bucket = slot_cap // seq_count
    target_dev = assignment // slot_cap
    within = assignment % slot_cap - seq_index * bucket
    bucket_row = target_dev * bucket + within
    token_send = jnp.where(live_mask[:, None] > 0, tokens, -1)
    partial_proj = jnp.dot(context, proj_quarter, preferred_element_type=jnp.float32)
    row_send = lax.psum_scatter(
        partial_proj.astype(jnp.bfloat16), "mp", scatter_dimension=1, tiled=True
    )
    buckets = jnp.zeros((slot_cap, row_send.shape[1]), jnp.bfloat16).at[bucket_row].set(row_send)
    token_buckets = (
        jnp.full((slot_cap, tokens.shape[1]), -1, jnp.int32).at[bucket_row].set(token_send)
    )
    arrived, token_arrived = (
        lax.all_to_all(
            lax.all_to_all(buckets, "seq", split_axis=0, concat_axis=0, tiled=True),
            "mp",
            split_axis=0,
            concat_axis=1,
            tiled=True,
        ),
        lax.all_to_all(
            lax.all_to_all(token_buckets, "seq", split_axis=0, concat_axis=0, tiled=True),
            "mp",
            split_axis=0,
            concat_axis=1,
            tiled=True,
        ),
    )
    depth_tokens = token_arrived[:, :CB]
    depth_live = (depth_tokens[:, 0] >= 0).astype(jnp.float32)
    depth_ids = jnp.maximum(depth_tokens, 0)

    def total_loss(hidden_in):
        per_frame = depth_losses(
            hidden_in,
            depth_ids,
            depth_live,
            query_full,
            key_full,
            value_full,
            out_full,
            logit_full,
            embed_full,
            gain_attn,
            gain_head,
        )
        return (jnp.sum(per_frame), per_frame)

    summed, pullback, slot_loss = jax.vjp(total_loss, arrived, has_aux=True)
    hidden_grad = pullback(jnp.ones((), jnp.float32))[0]
    returned = jax.tree.map(
        lambda part, own: part.astype(own.dtype),
        lax.all_to_all(
            lax.all_to_all(for_sending(hidden_grad), "mp", split_axis=1, concat_axis=0, tiled=True),
            "seq",
            split_axis=0,
            concat_axis=0,
            tiled=True,
        ),
        hidden_grad,
    )
    own_rows = jnp.take(returned, bucket_row, axis=0)
    hidden_rows = lax.all_gather(for_sending(own_rows), "mp", axis=1, tiled=True).astype(
        own_rows.dtype
    )
    context_grad = jnp.dot(hidden_rows, proj_quarter.T, preferred_element_type=jnp.float32).astype(
        jnp.bfloat16
    )
    return (context, context_grad, slot_loss)


def solution(mesh):
    placed = (
        P("seq", "mp"),
        P("seq", "mp"),
        P("seq", "mp"),
        P(),
        P("seq", None),
        P("seq"),
        P(("mp", "seq"), None),
        P("seq", None),
        P("seq", None),
        P("seq", None),
        P("seq", None),
        P("seq", None),
        P("seq", None),
        P(),
        P(),
    )
    return jax.shard_map(
        body,
        mesh=mesh,
        in_specs=placed,
        out_specs=(P("seq", "mp"), P("seq", "mp"), P(("seq", "mp"))),
        check_vma=False,
    )
```

profile of v0, /device:TPU:0, one launch (start us, length us, event | category | flops | bytes accessed | tf_op | source)
XLA Modules:
  0.0 416.2 jit_solution(15256508338967392261)
XLA Ops:
  8.0 1.0 copy.198
  9.0 1.1 fusion.54
  11.9 41.1 %all-gather.8.cloned.1.call-done = bf16[512,1024]{1,0:T(8,128)(2,1)} async-done(((bf16[64,1024]{1,0:T(8,128)(2,1)}), bf16[512,1024]{1,0:T(8,128)(2,1)}) %all-gather.8.cloned.1.call-update) | async-done | bytes 1048592 | tf_op jit(solution)/shard_map/all_gather | solution.py:143
  53.0 2.2 convolution_convert_fusion.11
  59.9 0.9 scatter_custom_fusion
  61.6 3.4 all-to-all-start
  66.3 5.0 %all-to-all-done = s32[8,1,128]{2,1,0:T(1,128)S(1)} async-done(((s32[8,1,128]{2,1,0:T(1,128)}), s32[8,1,128]{2,1,0:T(1,128)S(1)}, u32[]{:S(2)}, u32[]{:S(2)}) %all-to-all-start) | async-done | bytes 4128 | tf_op jit(solution)/shard_map/all_to_all | solution.py:169
  73.4 3.2 all-to-all-start.1
  77.2 3.2 all-to-all-done.1
  82.3 2.0 scatter_custom_fusion.1
  84.2 4.0 all-to-all-start.2
  88.3 9.9 %all-to-all-done.2 = bf16[8,32,256]{2,1,0:T(8,128)(2,1)} async-done(((bf16[8,32,256]{2,1,0:T(8,128)(2,1)}), bf16[8,32,256]{2,1,0:T(8,128)(2,1)}, u32[]{:S(2)}, u32[]{:S(2)}) %all-to-all-start.2) | async-done | bytes 131104 | tf_op jit(solution)/shard_map/all_to_all | solution.py:162
  98.2 3.5 all-to-all-start.3
  103.2 3.0 all-to-all-done.3
  106.2 21.7 %all-gather.10.cloned.1.call-done = bf16[1024,1024]{1,0:T(8,128)(2,1)} async-done(((bf16[128,1024]{1,0:T(8,128)(2,1)}), bf16[1024,1024]{1,0:T(8,128)(2,1)}) %all-gather.10.cloned.1.call-update) | async-done | bytes 2097168 | tf_op jit(solution)/shard_map/all_gather | solution.py:142
  127.9 3.2 gather_fusion
  133.2 35.6 %all-gather.14.cloned.1.call-done = bf16[1024,512]{1,0:T(8,128)(2,1)} async-done(((bf16[128,512]{1,0:T(8,128)(2,1)}), bf16[1024,512]{1,0:T(8,128)(2,1)}) %all-gather.14.cloned.1.call-update) | async-done | bytes 1048592 | tf_op jit(solution)/shard_map/all_gather | solution.py:137
  168.8 1.7 convolution_convert_fusion.9
  170.4 1.1 reshape.283
  171.5 38.4 %all-gather.16.cloned.1.call-done = bf16[1024,512]{1,0:T(8,128)(2,1)} async-done(((bf16[128,512]{1,0:T(8,128)(2,1)}), bf16[1024,512]{1,0:T(8,128)(2,1)}) %all-gather.16.cloned.1.call-update) | async-done | bytes 1048592 | tf_op jit(solution)/shard_map/all_gather | solution.py:138
  209.9 1.7 convolution_convert_fusion.8
  211.6 1.1 reshape.284
  212.7 1.9 fusion.30
  214.5 1.3 copy.172
  215.9 0.9 multiply_reduce_fusion.5
  216.8 0.9 copy.178
  218.0 33.2 %all-gather.12.cloned.1.call-done = bf16[1024,512]{1,0:T(8,128)(2,1)} async-done(((bf16[128,512]{1,0:T(8,128)(2,1)}), bf16[1024,512]{1,0:T(8,128)(2,1)}) %all-gather.12.cloned.1.call-update) | async-done | bytes 1048592 | tf_op jit(solution)/shard_map/all_gather | solution.py:139
  251.1 1.7 convolution_convert_fusion.10
  253.1 1.9 divide_convert_fusion
  255.4 1.3 reshape.280
  256.7 35.7 %all-gather.18.cloned.1.call-done = bf16[512,1024]{1,0:T(8,128)(2,1)} async-done(((bf16[64,1024]{1,0:T(8,128)(2,1)}), bf16[512,1024]{1,0:T(8,128)(2,1)}) %all-gather.18.cloned.1.call-update) | async-done | bytes 1048592 | tf_op jit(solution)/shard_map/all_gather | solution.py:140
  292.4 2.1 multiply_reduce_fusion.3
  295.1 47.7 %all-gather.20.cloned.1.call-done = bf16[1024,1024]{1,0:T(8,128)(2,1)} async-done(((bf16[128,1024]{1,0:T(8,128)(2,1)}), bf16[1024,1024]{1,0:T(8,128)(2,1)}) %all-gather.20.cloned.1.call-update) | async-done | bytes 2097168 | tf_op jit(solution)/shard_map/all_gather | solution.py:141
  342.8 2.6 exponential_reduce_fusion
  345.5 0.9 multiply_reduce_fusion.2
  346.7 1.0 copy-done.1
  348.5 3.1 fusion.13
  351.6 1.8 fusion.5
  353.3 1.7 copy.181
  355.2 2.4 multiply_reduce_fusion.1
  357.9 0.9 copy.188
  358.8 2.6 fusion.7
  361.4 2.7 fusion.6
  364.1 1.3 reshape.286
  365.4 1.1 copy.190
  366.5 1.0 reshape.289
  367.5 1.1 copy.179
  368.6 1.0 reshape.287
  369.7 1.1 copy.187
  370.8 1.0 reshape.288
  371.8 1.6 convolution_convert_fusion.1
  373.4 1.4 fusion.2
  374.9 1.4 fusion.4
  376.3 1.5 reshape.293
  378.7 2.6 fusion.12
  382.0 4.0 all-to-all-start.4
  386.0 2.3 gather_fusion.2
  388.7 1.9 all-to-all-done.4
  390.7 3.4 all-to-all-start.5
  394.8 1.2 bitcast_select_fusion
  396.0 5.4 %all-to-all-done.5 = bf16[8,32,256]{2,1,0:T(8,128)(2,1)S(1)} async-done(((bf16[8,32,256]{2,1,0:T(8,128)(2,1)}), bf16[8,32,256]{2,1,0:T(8,128)(2,1)S(1)}, u32[]{:S(2)}, u32[]{:S(2)}) %all-to-all-start.5) | async-done | bytes 131104 | tf_op jit(solution)/shard_map/all_to_all | solution.py:200
  401.4 1.0 gather_fusion.1
  402.4 5.8 %all_gather.31 = bf16[128,1024]{1,0:T(8,128)(2,1)S(1)} all-gather(bf16[128,256]{1,0:T(8,128)(2,1)S(1)} %broadcast_select_fusion.1), channel_id=1, replica_groups=mesh['seq'=8,'mp'=4] {'mp'}, dimensions={1}, use_global_device_ids=true | all-gather | bytes 327680 | tf_op jit(solution)/shard_map/all_gather | solution.py:210
  408.2 1.1 convolution_convert_fusion.12
  (161 shorter events, 22.7 us)
Async XLA Ops:
  7.2 1.9 copy-start
  7.2 3.4 copy-start.33
  7.2 45.8 %all-gather.8.cloned.1.call-start = ((), (), s32[]{:S(2)}) async-start(), calls=%async_computation.7 | async-start | bytes 1179648 | tf_op jit(solution)/shard_map/all_gather | solution.py:143
  7.9 74.4 %reduce-scatter.2.cloned.1.call-start = ((), (), s32[]{:S(2)}) async-start(), calls=%async_computation.8 | async-start | bytes 327680 | tf_op jit(solution)/shard_map/reduce_scatter | solution.py:153
  10.2 49.0 %copy-start.31 = (s32[128,4]{0,1:T(4,128)S(1)}, s32[128,4]{0,1:T(4,128)}, u32[]{:S(2)}) copy-start(s32[128,4]{0,1:T(4,128)} %param.19) | copy-start | bytes 6148
  10.2 49.1 %copy-start.32 = (s32[128]{0:T(128)S(1)}, s32[128]{0:T(128)}, u32[]{:S(2)}) copy-start(s32[128]{0:T(128)} %param.20) | copy-start | bytes 1540
  11.9 90.6 %copy-start.14 = (bf16[128,512]{1,0:T(8,128)(2,1)}, bf16[128,512]{1,0:T(8,128)(2,1)S(1)}, u32[]{:S(2)}) copy-start(bf16[128,512]{1,0:T(8,128)(2,1)S(1)} %multiply_convert_fusion.3) | copy-start | bytes 393220
  55.3 72.6 %all-gather.10.cloned.1.call-start = ((), (), s32[]{:S(2)}) async-start(), calls=%async_computation.9 | async-start | bytes 2359296 | tf_op jit(solution)/shard_map/all_gather | solution.py:142
  56.0 112.7 %all-gather.14.cloned.1.call-start = ((), (), s32[]{:S(2)}) async-start(), calls=%async_computation.11 | async-start | bytes 1179648 | tf_op jit(solution)/shard_map/all_gather | solution.py:137
  56.6 153.3 %all-gather.16.cloned.1.call-start = ((), (), s32[]{:S(2)}) async-start(), calls=%async_computation.12 | async-start | bytes 1179648 | tf_op jit(solution)/shard_map/all_gather | solution.py:138
  57.2 193.9 %all-gather.12.cloned.1.call-start = ((), (), s32[]{:S(2)}) async-start(), calls=%async_computation.10 | async-start | bytes 1179648 | tf_op jit(solution)/shard_map/all_gather | solution.py:139
  57.8 234.6 %all-gather.18.cloned.1.call-start = ((), (), s32[]{:S(2)}) async-start(), calls=%async_computation.13 | async-start | bytes 1179648 | tf_op jit(solution)/shard_map/all_gather | solution.py:140
  61.6 9.7 %all-to-all-start = ((s32[8,1,128]{2,1,0:T(1,128)}), s32[8,1,128]{2,1,0:T(1,128)S(1)}, u32[]{:S(2)}, u32[]{:S(2)}) async-start(s32[8,1,128]{2,1,0:T(1,128)} %reshape.344), calls=%async_computation | async-start | bytes 8192 | tf_op jit(solution)/shard_map/all_to_all | solution.py:169
  65.0 277.8 %all-gather.20.cloned.1.call-start = ((), (), s32[]{:S(2)}) async-start(), calls=%async_computation.14 | async-start | bytes 2359296 | tf_op jit(solution)/shard_map/all_gather | solution.py:141
  73.4 7.0 %all-to-all-start.1 = ((s32[4,1,256]{2,1,0:T(1,128)}), s32[4,1,256]{2,1,0:T(1,128)S(1)}, u32[]{:S(2)}, u32[]{:S(2)}) async-start(s32[4,1,256]{2,1,0:T(1,128)} %reshape.346), calls=%async_computation.1 | async-start | bytes 8192 | tf_op jit(solution)/shard_map/all_to_all | solution.py:168
  81.2 17.0 %copy-start.26 = (s32[4,4,64]{2,1,0:T(4,128)}, s32[4,4,64]{2,1,0:T(4,128)S(1)}, u32[]{:S(2)}) copy-start(s32[4,4,64]{2,1,0:T(4,128)S(1)} %reshape.347) | copy-start | bytes 12292
  84.2 14.0 %all-to-all-start.2 = ((bf16[8,32,256]{2,1,0:T(8,128)(2,1)}), bf16[8,32,256]{2,1,0:T(8,128)(2,1)}, u32[]{:S(2)}, u32[]{:S(2)}) async-start(bf16[8,32,256]{2,1,0:T(8,128)(2,1)} %bitcast.10), calls=%async_computation.3 | async-start | bytes 262144 | tf_op jit(solution)/shard_map/all_to_all | solution.py:162
  98.2 7.9 %all-to-all-start.3 = ((bf16[4,64,256]{2,1,0:T(8,128)(2,1)}), bf16[4,64,256]{2,1,0:T(8,128)(2,1)S(1)}, u32[]{:S(2)}, u32[]{:S(2)}) async-start(bf16[4,64,256]{2,1,0:T(8,128)(2,1)} %bitcast.11), calls=%async_computation.4 | async-start | bytes 262144 | tf_op jit(solution)/shard_map/all_to_all | solution.py:161
  131.1 1.4 copy-start.21
  132.4 0.7 copy-start.24
  132.5 0.6 copy-start.15
  217.8 37.2 %copy-start.12 = (bf16[64,8,4,4]{2,3,1,0:T(4,128)(2,1)}, bf16[64,8,4,4]{2,3,1,0:T(4,128)(2,1)S(1)}, u32[]{:S(2)}) copy-start(bf16[64,8,4,4]{2,3,1,0:T(4,128)(2,1)S(1)} %copy.178) | copy-start | bytes 49156
  217.9 37.0 %copy-start.17 = (f32[64,4,8]{1,2,0:T(8,128)}, f32[64,4,8]{1,2,0:T(8,128)S(1)}, u32[]{:S(2)}) copy-start(f32[64,4,8]{1,2,0:T(8,128)S(1)} %copy.175) | copy-start | bytes 24580
  253.1 1.9 copy-start.11
  256.7 86.1 %copy-start.20 = (f32[1024]{0:T(1024)S(1)}, f32[1024]{0:T(1024)}, u32[]{:S(2)}) copy-start(f32[1024]{0:T(1024)} %param.29) | copy-start | bytes 12292
  342.8 2.6 copy-start.29
  342.8 2.6 copy-start.3
  342.8 2.6 copy-start.28
  346.4 1.4 copy-start.7
  346.7 1.0 copy-start.1
  348.4 3.1 copy-start.13
  348.5 3.1 copy-start.18
  351.5 3.5 copy-start.19
  353.3 4.4 %copy-start.10 = (f32[64,8,4,4]{0,1,3,2:T(8,128)S(1)}, f32[64,8,4,4]{0,1,3,2:T(8,128)}, u32[]{:S(2)}) copy-start(f32[64,8,4,4]{0,1,3,2:T(8,128)} %copy.172) | copy-start | bytes 98308
  353.3 4.4 %copy-start.23 = (f32[4,4]{1,0:T(4,128)S(1)}, f32[4,4]{1,0:T(4,128)}, u32[]{:S(2)}) copy-start(f32[4,4]{1,0:T(4,128)} %fusion.44) | copy-start | bytes 196
  358.8 5.3 %copy-start.2 = (f32[256,1024]{1,0:T(8,128)S(1)}, f32[256,1024]{1,0:T(8,128)}, u32[]{:S(2)}) copy-start(f32[256,1024]{1,0:T(8,128)} %copy-done.1) | copy-start | bytes 3145732
  366.5 5.3 %copy-start.4 = (bf16[1024,512]{1,0:T(8,128)(2,1)S(1)}, bf16[1024,512]{1,0:T(8,128)(2,1)}, u32[]{:S(2)}) copy-start(bf16[1024,512]{1,0:T(8,128)(2,1)} %all-gather.16.cloned.1.call-done) | copy-start | bytes 3145732
  371.8 1.6 copy-start.5
  371.8 3.0 copy-start.8
  371.8 3.0 copy-start.9
  374.9 3.0 copy-start.22
  376.3 2.3 copy-start.25
  376.3 2.4 copy-start.16
  378.5 7.5 %copy-start.27 = (s32[256,2]{0,1:T(2,128)S(1)}, s32[256,2]{0,1:T(2,128)}, u32[]{:S(2)}) copy-start(s32[256,2]{0,1:T(2,128)} %add_bitcast_fusion) | copy-start | bytes 6148
  381.4 21.0 %copy-start.30 = (pred[128]{0:T(512)(128)(4,1)S(1)}, pred[128]{0:T(512)(128)(4,1)}, u32[]{:S(2)}) copy-start(pred[128]{0:T(512)(128)(4,1)} %get-tuple-element.3) | copy-start | bytes 388
  381.4 26.9 %copy-start.6 = (bf16[512,1024]{1,0:T(8,128)(2,1)S(1)}, bf16[512,1024]{1,0:T(8,128)(2,1)}, u32[]{:S(2)}) copy-start(bf16[512,1024]{1,0:T(8,128)(2,1)} %all-gather.8.cloned.1.call-done) | copy-start | bytes 3145732
  382.0 8.7 %all-to-all-start.4 = ((bf16[64,4,256]{2,0,1:T(8,128)(2,1)}), bf16[64,4,256]{2,0,1:T(8,128)(2,1)}, u32[]{:S(2)}, u32[]{:S(2)}) async-start(bf16[64,4,256]{2,0,1:T(8,128)(2,1)} %bitcast.109), calls=%async_computation.5 | async-start | bytes 262144 | tf_op jit(solution)/shard_map/all_to_all | solution.py:201
  390.7 10.7 %all-to-all-start.5 = ((bf16[8,32,256]{2,1,0:T(8,128)(2,1)}), bf16[8,32,256]{2,1,0:T(8,128)(2,1)S(1)}, u32[]{:S(2)}, u32[]{:S(2)}) async-start(bf16[8,32,256]{2,1,0:T(8,128)(2,1)} %bitcast.21), calls=%async_computation.6 | async-start | bytes 262144 | tf_op jit(solution)/shard_map/all_to_all | solution.py:200
Sparse Core Ops, SparseCore 0:
  10.2 42.8 all-gather.7
  55.5 18.7 reduce-scatter.1
  76.7 51.1 all-gather.9
  130.1 38.6 all-gather.13
  171.0 38.8 all-gather.15
  212.1 38.9 all-gather.11
  253.5 38.8 all-gather.17
  294.7 48.0 all-gather.19
where the time goes:
time: 418 us; the launch traced here: 416 us
  waiting for transfers between devices  286 us (68%)
  local copies, waits for them, and re-layouts  36.8 us (9%)
  matrix products  34.1 us (8%)
  starting transfers between devices  21.7 us (5%)
  other arithmetic  16.6 us (4%)
  between operations  14.9 us (4%)
  blocking collectives  5.79 us (1%)
    all_gather x1, waiting for transfers between devices, body(): lax.all_gather(logit_weight, 'seq', axis=0, tiled=True)  47.7 us
    all_gather x1, waiting for transfers between devices, body(): lax.all_gather(proj_weight, 'seq', axis=0, tiled=True)  41.1 us
    all_gather x1, waiting for transfers between devices, body(): lax.all_gather(key_weight, 'seq', axis=0, tiled=True)  38.4 us
    all_gather x1, waiting for transfers between devices, body(): lax.all_gather(out_weight, 'seq', axis=0, tiled=True)  35.7 us
    all_gather x1, waiting for transfers between devices, body(): lax.all_gather(query_weight, 'seq', axis=0, tiled=True)  35.6 us
    all_gather x1, waiting for transfers between devices, body(): lax.all_gather(value_weight, 'seq', axis=0, tiled=True)  33.2 us
    all_gather x1, waiting for transfers between devices, body(): lax.all_gather(embedding, 'seq', axis=0, tiled=True)  21.7 us
    all_to_all x1, waiting for transfers between devices, body(): lax.all_to_all(buckets, 'seq', split_axis=0, concat_axis=0, tiled=True)  9.92 us
  transfers between devices with their start and end apart: 14, of which 13 were waited for; matrix products, arithmetic and copies ran while one was open for 11% of the time, Pallas kernels for 0%

commit v1 on v0

--- a/solution.py
+++ b/solution.py
@@ -1,8 +1,11 @@
+import functools
 import math
 
 import jax
 import jax.numpy as jnp
 from jax import lax
+from jax.experimental import pallas as pl
+from jax.experimental.pallas import tpu as pltpu
 from jax.sharding import PartitionSpec as P
 
 HEAD_D = 64
@@ -11,14 +14,6 @@
 
 
 NORM_EPS = 1e-05
-
-
-def for_sending(value):
-
-    def short(part):
-        return part.astype(jnp.bfloat16) if part.dtype == jnp.float32 else part
-
-    return jax.tree.map(short, value)
 
 
 def rms_scale(inputs, gain):
@@ -88,6 +83,155 @@
     target = jnp.take_along_axis(logits, token_ids.reshape(row_count, 1), axis=1)[:, 0]
     per_frame = jnp.sum((log_total - target).reshape(frame_count, CB), axis=1)
     return per_frame * live_mask
+
+
+MESH = pl.DeviceIdType.MESH
+
+
+def gather_kernel(line, *refs):
+    count = (len(refs) - 3) // 2
+    shards, wholes = refs[:count], refs[count : 2 * count]
+    send_sem, recv_sem, local_sem = refs[2 * count :]
+    seq, mp = lax.axis_index("seq"), lax.axis_index("mp")
+    zi, yi = seq // 2, seq % 2
+    xi, ci = mp // 2, mp % 2
+    z_peers = [lax.rem(zi + d, line) * 2 + yi for d in range(1, line)]
+    y_peer = zi * 2 + (1 - yi)
+    x_peer = (1 - xi) * 2 + ci
+    c_peer = xi * 2 + (1 - ci)
+
+    barrier = pltpu.get_barrier_semaphore()
+    greeted = [(peer, mp) for peer in z_peers] + [(y_peer, mp), (seq, x_peer), (seq, c_peer)]
+    for peer in greeted:
+        pl.semaphore_signal(barrier, inc=1, device_id=peer, device_id_type=MESH)
+    pl.semaphore_wait(barrier, len(greeted))
+
+    near = [lax.rem(zi + line - d, line) * 2 + yi for d in range(line)]
+    far = [lax.rem(zi + line - d, line) * 2 + (1 - yi) for d in range(line)]
+    others = near[1:] + far
+
+    def rows_of(number, source, quarter):
+        rows = shards[number].shape[0]
+        if number == 0:
+            return pl.ds(pl.multiple_of(source * rows, rows), rows)
+        part = rows // 4
+        return pl.ds(pl.multiple_of(source * rows + quarter * part, part), part)
+
+    sends = []
+
+    def send(number, rows, slot, peer, src=None):
+        copy = pltpu.make_async_remote_copy(
+            src_ref=wholes[number].at[rows, :] if src is None else src,
+            dst_ref=wholes[number].at[rows, :],
+            send_sem=send_sem.at[number, slot],
+            recv_sem=recv_sem.at[number, slot],
+            device_id=peer,
+            device_id_type=MESH,
+        )
+        copy.start()
+        sends.append(copy)
+
+    def arrived(number, rows, slot):
+        here = wholes[number].at[rows, :]
+        pltpu.make_async_remote_copy(
+            src_ref=here,
+            dst_ref=here,
+            send_sem=send_sem.at[number, slot],
+            recv_sem=recv_sem.at[number, slot],
+            device_id=(seq, mp),
+            device_id_type=MESH,
+        ).wait_recv()
+
+    z_at = 0
+    y_at = line - 1
+    x_at = y_at + line
+    c_at = x_at + 2 * line - 1
+    xc_at = c_at + 2 * line - 1
+
+    own_copies = []
+    for number in range(count):
+        rows = shards[number].shape[0]
+        if number == 0:
+            own = shards[number]
+        else:
+            part = rows // 4
+            own = shards[number].at[pl.ds(pl.multiple_of(mp * part, part), part), :]
+        target = rows_of(number, seq, mp)
+        for d in range(1, line):
+            send(number, target, z_at + d - 1, (z_peers[d - 1], mp), own)
+        send(number, target, y_at, (y_peer, mp), own)
+    for number in range(count):
+        rows = shards[number].shape[0]
+        copy = pltpu.make_async_copy(
+            shards[number],
+            wholes[number].at[pl.ds(pl.multiple_of(seq * rows, rows), rows), :],
+            local_sem.at[number],
+        )
+        copy.start()
+        own_copies.append(copy)
+
+    def share(number, rows, at):
+        if number > 0:
+            send(number, rows, x_at + at, (seq, x_peer))
+            send(number, rows, c_at + at, (seq, c_peer))
+
+    def first_hops(number):
+        for d in range(1, line):
+            rows = rows_of(number, near[d], mp)
+            arrived(number, rows, z_at + d - 1)
+            send(number, rows, y_at + d, (y_peer, mp))
+            share(number, rows, d - 1)
+        for d in range(line):
+            rows = rows_of(number, far[d], mp)
+            arrived(number, rows, y_at + d)
+            share(number, rows, line - 1 + d)
+
+    def cross_hops(number):
+        for at, source in enumerate(others):
+            rows = rows_of(number, source, x_peer)
+            arrived(number, rows, x_at + at)
+            send(number, rows, xc_at + at, (seq, c_peer))
+
+    for number in range(count):
+        first_hops(number)
+        if number > 1:
+            cross_hops(number - 1)
+    cross_hops(count - 1)
+    diagonal = (1 - xi) * 2 + (1 - ci)
+    for number in range(1, count):
+        for at, source in enumerate(others):
+            arrived(number, rows_of(number, source, c_peer), c_at + at)
+            arrived(number, rows_of(number, source, diagonal), xc_at + at)
+    for copy in own_copies:
+        copy.wait()
+    for copy in sends:
+        copy.wait_send()
+
+
+def gather_all(private, shared):
+    seq_count = lax.axis_size("seq")
+    shards = (private,) + shared
+    small = private.shape[0] % 16 or any(part.shape[0] % 64 for part in shared)
+    if small or seq_count != 8 or lax.axis_size("mp") != 4:
+        return tuple(lax.all_gather(part, "seq", axis=0, tiled=True) for part in shards)
+    line = seq_count // 2
+    slots = (line - 1) + line + 3 * (2 * line - 1)
+    count = len(shards)
+    return pl.pallas_call(
+        functools.partial(gather_kernel, line),
+        out_shape=tuple(
+            jax.ShapeDtypeStruct((part.shape[0] * seq_count, part.shape[1]), part.dtype)
+            for part in shards
+        ),
+        in_specs=[pl.BlockSpec(memory_space=pl.ANY)] * count,
+        out_specs=tuple([pl.BlockSpec(memory_space=pl.ANY)] * count),
+        scratch_shapes=[
+            pltpu.SemaphoreType.DMA((count, slots)),
+            pltpu.SemaphoreType.DMA((count, slots)),
+            pltpu.SemaphoreType.DMA((count,)),
+        ],
+        compiler_params=pltpu.CompilerParams(collective_id=0, has_side_effects=True),
+    )(*shards)
 
 
 def body(
@@ -133,55 +277,36 @@
     mixture = mixture / jnp.transpose(totals)[:, :, None]
     live_mask = (places < length).astype(jnp.float32)
     context = (mixture.reshape(frame_count, local_width) * live_mask[:, None]).astype(jnp.bfloat16)
-    gathered = (
-        lax.all_gather(query_weight, "seq", axis=0, tiled=True),
-        lax.all_gather(key_weight, "seq", axis=0, tiled=True),
-        lax.all_gather(value_weight, "seq", axis=0, tiled=True),
-        lax.all_gather(out_weight, "seq", axis=0, tiled=True),
-        lax.all_gather(logit_weight, "seq", axis=0, tiled=True),
-        lax.all_gather(embedding, "seq", axis=0, tiled=True),
-        lax.all_gather(proj_weight, "seq", axis=0, tiled=True),
-    )
-    query_full, key_full, value_full, out_full, logit_full, embed_full, proj_quarter = gathered
-    slot_cap = 2 * frame_count
-    bucket = slot_cap // seq_count
-    target_dev = assignment // slot_cap
-    within = assignment % slot_cap - seq_index * bucket
-    bucket_row = target_dev * bucket + within
-    token_send = jnp.where(live_mask[:, None] > 0, tokens, -1)
+    proj_quarter, embed_full, qkv_full, out_full, logit_full = gather_all(
+        proj_weight,
+        (
+            embedding,
+            jnp.concatenate([query_weight, key_weight, value_weight], axis=1),
+            out_weight,
+            logit_weight,
+        ),
+    )
+    query_full, key_full, value_full = jnp.split(qkv_full, 3, axis=1)
+    mp_count = lax.axis_size("mp")
+    mp_index = lax.axis_index("mp")
+    share = frame_count // mp_count
+    first = mp_index * share
     partial_proj = jnp.dot(context, proj_quarter, preferred_element_type=jnp.float32)
-    row_send = lax.psum_scatter(
-        partial_proj.astype(jnp.bfloat16), "mp", scatter_dimension=1, tiled=True
-    )
-    buckets = jnp.zeros((slot_cap, row_send.shape[1]), jnp.bfloat16).at[bucket_row].set(row_send)
-    token_buckets = (
-        jnp.full((slot_cap, tokens.shape[1]), -1, jnp.int32).at[bucket_row].set(token_send)
-    )
-    arrived, token_arrived = (
-        lax.all_to_all(
-            lax.all_to_all(buckets, "seq", split_axis=0, concat_axis=0, tiled=True),
-            "mp",
-            split_axis=0,
-            concat_axis=1,
-            tiled=True,
-        ),
-        lax.all_to_all(
-            lax.all_to_all(token_buckets, "seq", split_axis=0, concat_axis=0, tiled=True),
-            "mp",
-            split_axis=0,
-            concat_axis=1,
-            tiled=True,
-        ),
-    )
-    depth_tokens = token_arrived[:, :CB]
-    depth_live = (depth_tokens[:, 0] >= 0).astype(jnp.float32)
-    depth_ids = jnp.maximum(depth_tokens, 0)
+    parts = lax.all_to_all(
+        partial_proj.astype(jnp.bfloat16).reshape(mp_count, share, -1),
+        "mp",
+        split_axis=0,
+        concat_axis=0,
+    )
+    hidden = jnp.sum(parts.astype(jnp.float32), axis=0).astype(jnp.bfloat16)
+    own_tokens = lax.dynamic_slice_in_dim(tokens, first, share)
+    own_live = lax.dynamic_slice_in_dim(live_mask, first, share)
 
     def total_loss(hidden_in):
         per_frame = depth_losses(
             hidden_in,
-            depth_ids,
-            depth_live,
+            own_tokens,
+            own_live,
             query_full,
             key_full,
             value_full,
@@ -193,25 +318,18 @@
         )
         return (jnp.sum(per_frame), per_frame)
 
-    summed, pullback, slot_loss = jax.vjp(total_loss, arrived, has_aux=True)
+    summed, pullback, own_loss = jax.vjp(total_loss, hidden, has_aux=True)
     hidden_grad = pullback(jnp.ones((), jnp.float32))[0]
-    returned = jax.tree.map(
-        lambda part, own: part.astype(own.dtype),
-        lax.all_to_all(
-            lax.all_to_all(for_sending(hidden_grad), "mp", split_axis=1, concat_axis=0, tiled=True),
-            "seq",
-            split_axis=0,
-            concat_axis=0,
-            tiled=True,
-        ),
-        hidden_grad,
-    )
-    own_rows = jnp.take(returned, bucket_row, axis=0)
-    hidden_rows = lax.all_gather(for_sending(own_rows), "mp", axis=1, tiled=True).astype(
-        own_rows.dtype
-    )
+    hidden_rows = lax.all_gather(hidden_grad, "mp", axis=0, tiled=True)
     context_grad = jnp.dot(hidden_rows, proj_quarter.T, preferred_element_type=jnp.float32).astype(
         jnp.bfloat16
+    )
+    frame_loss = lax.all_gather(own_loss, ("seq", "mp"), axis=0, tiled=True)
+    frame_slot = lax.all_gather(assignment, "seq", axis=0, tiled=True)
+    slot_count = 2 * share
+    slots = (seq_index * mp_count + mp_index) * slot_count + jnp.arange(slot_count)
+    slot_loss = jnp.sum(
+        jnp.where(frame_slot[None, :] == slots[:, None], frame_loss[None, :], 0.0), axis=1
     )
     return (context, context_grad, slot_loss)
 

time: 418 us -> 197 us (0.47)
  waiting for transfers between devices: 286 us -> 0.01 us
  Pallas kernels: 0 us -> 71.3 us
  blocking collectives: 5.79 us -> 64.7 us
  starting transfers between devices: 21.7 us -> 3.4 us
  local copies, waits for them, and re-layouts: 36.8 us -> 19 us
  between operations: 14.9 us -> 1.41 us
  matrix products: 34.1 us -> 23.2 us
  other arithmetic: 16.6 us -> 12.1 us
    all_gather x7 -> x0, waiting for transfers between devices: 253 us -> none  [the longest x1 47.7 us: body(): lax.all_gather(logit_weight, 'seq', axis=0, tiled=True)]
    pallas_call x0 -> x1, Pallas kernels: none -> 71.3 us  [gather_all(): pl.pallas_call(functools.partial(gather_kernel, line), out_shape=tuple((j...]
    unnamed x0 -> x1, blocking collectives: none -> 36.9 us
    all_to_all x6 -> x1, waiting for transfers between devices: 28.5 us -> 0.01 us  [body(): lax.all_to_all(partial_proj.astype(jnp.bfloat16).reshape(mp_count, share,...]
    all_gather x1 -> x2, blocking collectives: 5.79 us -> 27.8 us  [the longest x1 21.6 us: body(): frame_slot = lax.all_gather(assignment, 'seq', axis=0, tiled=True)]
    all_to_all x6 -> x1, starting transfers between devices: 21.4 us -> 3.4 us  [body(): lax.all_to_all(partial_proj.astype(jnp.bfloat16).reshape(mp_count, share,...]
    dot_general x3, matrix products: 7.16 us -> 1.32 us  [depth_losses(): jnp.einsum('fqhd,fkhd->fhqk', query_rows, key_rows, preferred_element_typ...]
    unnamed x8 -> x0, waiting for transfers between devices: 4.35 us -> none
  transfers between devices with their start and end apart: 14 -> 1, of which waited for: 13 -> 0; matrix products, arithmetic and copies ran while one was open for 11% -> 1% of each run, Pallas kernels for 0% -> 0%
where the time goes in v1:
time: 197 us; the launch traced here: 195 us
  Pallas kernels  71.3 us (36%)
  blocking collectives  64.7 us (33%)
  matrix products  23.2 us (12%)
  local copies, waits for them, and re-layouts  19 us (10%)
  other arithmetic  12.1 us (6%)
  starting transfers between devices  3.4 us (2%)
    pallas_call x1, Pallas kernels, gather_all(): pl.pallas_call(functools.partial(gather_kernel, line), out_shape=tuple((j...  71.3 us
    unnamed x1, blocking collectives  36.9 us
    all_gather x1, blocking collectives, body(): frame_slot = lax.all_gather(assignment, 'seq', axis=0, tiled=True)  21.6 us
    all_gather x1, blocking collectives, body(): hidden_rows = lax.all_gather(hidden_grad, 'mp', axis=0, tiled=True)  6.22 us
  transfers between devices with their start and end apart: 1, of which 0 were waited for; matrix products, arithmetic and copies ran while one was open for 1% of the time, Pallas kernels for 0%

profile of v1, /device:TPU:0, one launch (start us, length us, event | category | flops | bytes accessed | tf_op | source)
XLA Modules:
  0.0 195.1 jit_solution(9289596767528656778)
XLA Ops:
  0.7 1.3 dynamic_slice.9
  1.9 0.6 compare_convert_fusion
  2.6 1.0 copy.154
  3.7 1.1 fusion.51
  5.2 1.8 pad_maximum_fusion.refs_2_
  7.1 71.3 %shard_map.166 = (bf16[512,1024]{1,0:T(8,128)(2,1)}, bf16[1024,1024]{1,0:T(8,128)(2,1)}, bf16[1024,1536]{1,0:T(8,128)(2,1)}, bf16[512,1024]{1,0:T(8,128)(2,1)}, bf16[1024,1024]{1,0:T(8,128)(2,1)}) custom-call(bf16[64,1024]{1,0:T(8,128)(2,1)} %refs_0_.1, bf16[128,1024]{1,0:T(8,128)(2,1)} %refs_1_.1, bf16[128,1536]{1,0:T(8,128)(2,1)} %pad_maximum_fusion.refs_2_, ...), custom_call_target="tpu_custom_call" | custom-call | tf_op jit(solution)/shard_map/pallas_call | solution.py:220
  78.4 2.4 %convolution_convert_fusion.7 = bf16[128,1024]{1,0:T(8,128)(2,1)} fusion(bf16[128,512]{1,0:T(8,128)(2,1)S(1)} %multiply_convert_fusion.3, bf16[512,1024]{1,0:T(8,128)(2,1)} %get-tuple-element.8), kind=kOutput, calls=%fused_computation.13 | convolution fusion | flops 134348800 | bytes 1441792 | tf_op jit(solution)/shard_map/dot_general | solution.py:294
  80.8 3.4 %all-to-all-start = ((bf16[4,32,1024]{2,1,0:T(8,128)(2,1)}), bf16[4,32,1024]{2,1,0:T(8,128)(2,1)S(1)}, u32[]{:S(2)}, u32[]{:S(2)}) async-start(bf16[4,32,1024]{2,1,0:T(8,128)(2,1)} %bitcast.5), calls=%async_computation | async-start | bytes 524288 | tf_op jit(solution)/shard_map/all_to_all | solution.py:295
  84.8 0.2 copy-done.9
  85.0 0.8 gather_fusion
  86.0 0.5 iota_add_fusion
  86.6 21.6 %all-gather = s32[8,1,128]{2,1,0:T(1,128)} all-gather(s32[1,1,128]{2,1,0:T(1,128)S(1)} %bitcast.84), channel_id=1, replica_groups=mesh['seq'=8,'mp'=4] {'seq'}, dimensions={0}, use_global_device_ids=true | all-gather | bytes 4608 | tf_op jit(solution)/shard_map/all_gather | solution.py:328
  108.2 0.2 broadcast_select_fusion
  108.4 0.5 compare_select_fusion.3
  109.0 0.4 multiply_reduce_fusion.4
  109.5 0.3 multiply_convert_fusion.1
  109.8 0.3 copy-done.20
  110.2 1.5 convolution_convert_fusion.10
  111.7 1.5 convolution_convert_fusion.9
  113.3 1.5 convolution_convert_fusion.11
  115.3 0.4 fusion.36
  115.7 0.4 copy.132
  116.2 0.5 copy.138
  116.9 0.2 reshape.257
  117.2 0.3 copy-done.16
  117.6 0.7 copy-done.18
  118.3 1.4 divide_convert_fusion
  119.7 0.9 reshape.260
  120.8 1.7 multiply_reduce_fusion.3
  122.5 0.5 copy-done.34
  123.0 1.1 exponential_reduce_fusion
  124.1 2.0 %gather_fusion.1 = f32[128]{0:T(128)} fusion(f32[128,1024]{1,0:T(8,128)S(1)} %get-tuple-element.28, s32[128]{0:T(128)S(1)} %or_bitcast_fusion), kind=kCustom, calls=%fused_computation.1 | custom fusion | bytes 2048 | tf_op jit(solution)/shard_map/jvp(jit(take_along_axis))/gather | solution.py:83
  126.1 1.4 gather.12
  127.5 0.7 log.7
  128.1 0.7 log.8
  128.8 0.9 subtract_reduce_fusion
  129.7 0.9 multiply_dynamic-update-slice_fusion
  130.6 0.7 broadcast_in_dim.69
  131.3 1.4 reshape.253
  132.7 0.8 fusion.50
  133.5 1.5 multiply_reduce_fusion.2
  135.2 0.5 fusion.11
  136.0 0.5 fusion.2
  136.5 0.2 copy-done.19
  136.7 0.5 fusion.19
  137.3 0.2 copy-done.23
  137.5 0.4 copy.141
  138.0 0.7 multiply_reduce_fusion.1
  138.9 0.5 copy.148
  139.5 0.5 fusion.3
  140.0 0.4 fusion.4
  140.6 0.2 reshape.262
  140.9 0.2 reshape.263
  141.1 1.7 convolution_convert_fusion.2
  142.9 0.2 reshape.264
  143.1 1.7 convolution_convert_fusion
  144.8 1.8 fusion.10
  146.8 1.1 multiply_reduce_fusion
  147.9 0.7 multiply_multiply_fusion.1
  148.7 1.4 fusion.18
  150.1 6.2 %all_gather.9 = bf16[128,1024]{1,0:T(8,128)(2,1)S(1)} all-gather(bf16[32,1024]{1,0:T(8,128)(2,1)S(1)} %fusion.18), channel_id=1, replica_groups=mesh['seq'=8,'mp'=4] {'mp'}, dimensions={0}, use_global_device_ids=true | all-gather | bytes 327680 | tf_op jit(solution)/shard_map/all_gather | solution.py:323
  156.4 1.1 convolution_convert_fusion.8
  157.5 36.9 %all-reduce.1 = f32[1024]{0:T(1024)S(1)} all-reduce(f32[1024]{0:T(1024)S(1)} %copy-done.30), channel_id=1, replica_groups=mesh['seq'=8,'mp'=4] {'seq','mp'}, use_global_device_ids=true, to_apply=%add.1 | all-reduce | flops 1024 | bytes 8192
  194.4 0.7 select_reduce_fusion
  (117 shorter events, 3.9 us)
Async XLA Ops:
  0.6 3.0 %copy-start = (bf16[128,512]{1,0:T(8,128)(2,1)S(1)}, bf16[128,512]{1,0:T(8,128)(2,1)}, u32[]{:S(2)}) copy-start(bf16[128,512]{1,0:T(8,128)(2,1)} %param.16) | copy-start | bytes 393220
  2.6 4.5 %copy-start.32 = (f32[128]{0:T(128)}, f32[128]{0:T(128)S(1)}, u32[]{:S(2)}) copy-start(f32[128]{0:T(128)S(1)} %compare_convert_fusion) | copy-start | bytes 1540
  3.6 80.6 %copy-start.33 = (s32[128,4]{0,1:T(4,128)S(1)}, s32[128,4]{0,1:T(4,128)}, u32[]{:S(2)}) copy-start(s32[128,4]{0,1:T(4,128)} %param.19) | copy-start | bytes 6148
  5.2 75.6 %copy-start.11 = (bf16[128,512]{1,0:T(8,128)(2,1)}, bf16[128,512]{1,0:T(8,128)(2,1)S(1)}, u32[]{:S(2)}) copy-start(bf16[128,512]{1,0:T(8,128)(2,1)S(1)} %multiply_convert_fusion.3) | copy-start | bytes 393220
  7.1 79.5 %copy-start.36 = (s32[128]{0:T(128)S(1)}, s32[128]{0:T(128)}, u32[]{:S(2)}) copy-start(s32[128]{0:T(128)} %param.20) | copy-start | bytes 1540
  78.4 6.6 %copy-start.6 = (bf16[1024,1024]{1,0:T(8,128)(2,1)S(1)}, bf16[1024,1024]{1,0:T(8,128)(2,1)}, u32[]{:S(2)}) copy-start(bf16[1024,1024]{1,0:T(8,128)(2,1)} %get-tuple-element.9) | copy-start | bytes 6291460
  78.4 31.1 %copy-start.26 = (f32[1024]{0:T(1024)S(1)}, f32[1024]{0:T(1024)}, u32[]{:S(2)}) copy-start(f32[1024]{0:T(1024)} %param.28) | copy-start | bytes 12292
  80.8 28.1 %all-to-all-start = ((bf16[4,32,1024]{2,1,0:T(8,128)(2,1)}), bf16[4,32,1024]{2,1,0:T(8,128)(2,1)S(1)}, u32[]{:S(2)}, u32[]{:S(2)}) async-start(bf16[4,32,1024]{2,1,0:T(8,128)(2,1)} %bitcast.5), calls=%async_computation | async-start | bytes 524288 | tf_op jit(solution)/shard_map/all_to_all | solution.py:295
  84.4 0.6 copy-start.9
  109.0 5.9 %copy-start.4 = (f32[32,1024]{1,0:T(8,128)}, f32[32,1024]{1,0:T(8,128)S(1)}, u32[]{:S(2)}) copy-start(f32[32,1024]{1,0:T(8,128)S(1)} %convert_element_type.131) | copy-start | bytes 393220
  109.4 5.4 %copy-start.27 = (f32[32,4]{0,1:T(4,128)}, f32[32,4]{0,1:T(4,128)S(1)}, u32[]{:S(2)}) copy-start(f32[32,4]{0,1:T(4,128)S(1)} %copy.128) | copy-start | bytes 1540
  109.5 0.6 copy-start.20
  115.1 2.1 %copy-start.12 = (bf16[32,4,8,64]{3,2,1,0:T(8,128)(2,1)}, bf16[32,4,8,64]{3,2,1,0:T(8,128)(2,1)S(1)}, u32[]{:S(2)}) copy-start(bf16[32,4,8,64]{3,2,1,0:T(8,128)(2,1)S(1)} %reshape.258) | copy-start | bytes 393220
  115.3 1.9 copy-start.14
  116.1 1.1 copy-start.7
  116.2 0.6 copy-start.22
  116.8 0.7 copy-start.16
  116.9 0.6 copy-start.24
  117.6 0.7 copy-start.18
  119.7 3.4 %copy-start.1 = (bf16[1024,1024]{1,0:T(8,128)(2,1)S(1)}, bf16[1024,1024]{1,0:T(8,128)(2,1)}, u32[]{:S(2)}) copy-start(bf16[1024,1024]{1,0:T(8,128)(2,1)} %get-tuple-element.12) | copy-start | bytes 6291460
  119.7 3.4 %copy-start.31 = (f32[1024]{0:T(1024)S(1)}, f32[1024]{0:T(1024)}, u32[]{:S(2)}) copy-start(f32[1024]{0:T(1024)} %param.29) | copy-start | bytes 12292
  122.4 0.6 copy-start.34
  130.6 4.4 %copy-start.29 = (f32[1024]{0:T(1024)}, f32[1024]{0:T(1024)S(1)}, u32[]{:S(2)}) copy-start(f32[1024]{0:T(1024)S(1)} %get-tuple-element.13) | copy-start | bytes 12292
  132.7 2.3 %copy-start.35 = (f32[128]{0:T(128)S(1)}, f32[128]{0:T(128)}, u32[]{:S(2)}) copy-start(f32[128]{0:T(128)} %copy-done.34) | copy-start | bytes 1540
  132.7 2.5 %copy-start.2 = (bf16[512,1024]{1,0:T(8,128)(2,1)S(1)}, bf16[512,1024]{1,0:T(8,128)(2,1)}, u32[]{:S(2)}) copy-start(bf16[512,1024]{1,0:T(8,128)(2,1)} %get-tuple-element.11) | copy-start | bytes 3145732
  135.0 1.0 copy-start.17
  135.0 1.0 copy-start.25
  135.7 1.0 copy-start.19
  136.7 0.7 copy-start.23
  136.7 1.3 copy-start.10
  136.7 2.1 %copy-start.8 = (f32[32,8,4,4]{0,1,3,2:T(8,128)S(1)}, f32[32,8,4,4]{0,1,3,2:T(8,128)}, u32[]{:S(2)}) copy-start(f32[32,8,4,4]{0,1,3,2:T(8,128)} %copy-done.7) | copy-start | bytes 49156
  136.7 2.7 %copy-start.13 = (bf16[32,4,8,64]{3,2,1,0:T(8,128)(2,1)S(1)}, bf16[32,4,8,64]{3,2,1,0:T(8,128)(2,1)}, u32[]{:S(2)}) copy-start(bf16[32,4,8,64]{3,2,1,0:T(8,128)(2,1)} %copy-done.12) | copy-start | bytes 393220
  137.4 2.5 %copy-start.15 = (bf16[32,4,8,64]{3,2,1,0:T(8,128)(2,1)S(1)}, bf16[32,4,8,64]{3,2,1,0:T(8,128)(2,1)}, u32[]{:S(2)}) copy-start(bf16[32,4,8,64]{3,2,1,0:T(8,128)(2,1)} %copy-done.14) | copy-start | bytes 393220
  142.8 4.0 %copy-start.5 = (f32[32,1024]{1,0:T(8,128)S(1)}, f32[32,1024]{1,0:T(8,128)}, u32[]{:S(2)}) copy-start(f32[32,1024]{1,0:T(8,128)} %copy-done.4) | copy-start | bytes 393220
  142.9 5.9 %copy-start.21 = (f32[32,4]{1,0:T(8,128)S(1)}, f32[32,4]{1,0:T(8,128)}, u32[]{:S(2)}) copy-start(f32[32,4]{1,0:T(8,128)} %copy-done.20) | copy-start | bytes 1540
  144.8 11.6 %copy-start.3 = (bf16[512,1024]{1,0:T(8,128)(2,1)S(1)}, bf16[512,1024]{1,0:T(8,128)(2,1)}, u32[]{:S(2)}) copy-start(bf16[512,1024]{1,0:T(8,128)(2,1)} %get-tuple-element.8) | copy-start | bytes 3145732
  146.6 10.9 %copy-start.30 = (f32[1024]{0:T(1024)S(1)}, f32[1024]{0:T(1024)}, u32[]{:S(2)}) copy-start(f32[1024]{0:T(1024)} %copy-done.29) | copy-start | bytes 12292
  146.6 47.8 %copy-start.28 = (s32[8,1,128]{2,1,0:T(1,128)S(1)}, s32[8,1,128]{2,1,0:T(1,128)}, u32[]{:S(2)}) copy-start(s32[8,1,128]{2,1,0:T(1,128)} %all-gather) | copy-start | bytes 12292
  146.6 47.8 %copy-start.37 = (s32[64]{0:T(128)S(1)}, s32[64]{0:T(128)}, u32[]{:S(2)}) copy-start(s32[64]{0:T(128)} %iota_add_fusion) | copy-start | bytes 772

commit v2 on v1

--- a/solution.py
+++ b/solution.py
@@ -88,30 +88,170 @@
 MESH = pl.DeviceIdType.MESH
 
 
-def gather_kernel(line, *refs):
-    count = (len(refs) - 3) // 2
-    shards, wholes = refs[:count], refs[count : 2 * count]
-    send_sem, recv_sem, local_sem = refs[2 * count :]
+PAIRS = [(c, k) for c in range(CB) for k in range(c + 1)]
+
+
+def dot(left, right):
+    return jnp.dot(left, right, preferred_element_type=jnp.float32)
+
+
+def dot_turned(left, right):
+    return lax.dot_general(left, right, (((1,), (1,)), ((), ())), preferred_element_type=jnp.float32)
+
+
+def inverse_rms(rows):
+    return lax.rsqrt(jnp.mean(rows * rows, axis=-1, keepdims=True) + NORM_EPS)
+
+
+def rms_back(rows, scale, gain, grad):
+    turned = grad * gain
+    return scale * (turned - rows * (scale * scale) * jnp.mean(turned * rows, axis=-1, keepdims=True))
+
+
+def slab(rows, place):
+    size = rows.shape[0] // CB
+    return rows[place * size : (place + 1) * size]
+
+
+def head_sums(values):
+    width = values.shape[1]
+    left = lax.broadcasted_iota(jnp.int32, (width, width), 0) // HEAD_D
+    right = lax.broadcasted_iota(jnp.int32, (width, width), 1) // HEAD_D
+    ones = jnp.where(left == right, 1.0, 0.0).astype(jnp.bfloat16)
+    high = values.astype(jnp.bfloat16)
+    low = (values - high.astype(jnp.float32)).astype(jnp.bfloat16)
+    return dot(high, ones) + dot(low, ones)
+
+
+def temporal_head(query, key, value, live):
+    size = query.shape[0]
+    scores = dot_turned(query, key) / math.sqrt(HEAD_T)
+    visible = lax.broadcasted_iota(jnp.int32, (size, size), 1) <= lax.broadcasted_iota(
+        jnp.int32, (size, size), 0
+    )
+    weights = jnp.where(visible, jnp.exp(scores), 0.0)
+    totals = jnp.sum(weights, axis=-1, keepdims=True)
+    mixture = dot(weights.astype(jnp.bfloat16), value) / totals
+    return (mixture * live).astype(jnp.bfloat16)
+
+
+def chosen(ids, width):
+    return lax.broadcasted_iota(jnp.int32, (ids.shape[0], width), 1) == ids
+
+
+def depth_attention(qkv):
+    width = qkv.shape[1] // 3
+    query, key, value = (
+        qkv[:, at * width : (at + 1) * width].astype(jnp.float32) for at in range(3)
+    )
+    products = jnp.concatenate([slab(query, c) * slab(key, k) for c, k in PAIRS], axis=0)
+    weights = jnp.exp(head_sums(products) / math.sqrt(HEAD_D))
+    size = products.shape[0] // len(PAIRS)
+    parts = {pair: weights[at * size : (at + 1) * size] for at, pair in enumerate(PAIRS)}
+    rounded = {
+        pair: part.astype(jnp.bfloat16).astype(jnp.float32) for pair, part in parts.items()
+    }
+    totals = [sum(parts[c, k] for k in range(c + 1)) for c in range(CB)]
+    mixed = [
+        sum(rounded[c, k] * slab(value, k) for k in range(c + 1)) / totals[c] for c in range(CB)
+    ]
+    return jnp.concatenate(mixed, axis=0), (query, key, value, parts, rounded, totals)
+
+
+def depth_attention_back(grad, mixed, saved):
+    query, key, value, parts, rounded, totals = saved
+    down = [slab(grad, c) / totals[c] for c in range(CB)]
+    products = [down[c] * slab(value, k) for c, k in PAIRS]
+    products += [down[c] * slab(mixed, c) for c in range(CB)]
+    sums = head_sums(jnp.concatenate(products, axis=0))
+    size = grad.shape[0] // CB
+    pieces = [sums[at * size : (at + 1) * size] for at in range(len(products))]
+    back = {}
+    for at, (c, k) in enumerate(PAIRS):
+        weight_grad = pieces[at].astype(jnp.bfloat16).astype(jnp.float32)
+        back[c, k] = (weight_grad - pieces[len(PAIRS) + c]) * parts[c, k] / math.sqrt(HEAD_D)
+    query_grad = [sum(back[c, k] * slab(key, k) for k in range(c + 1)) for c in range(CB)]
+    key_grad = [sum(back[c, k] * slab(query, c) for c in range(k, CB)) for k in range(CB)]
+    value_grad = [sum(rounded[c, k] * down[c] for c in range(k, CB)) for k in range(CB)]
+    return jnp.concatenate(
+        [jnp.concatenate(part, axis=0) for part in (query_grad, key_grad, value_grad)], axis=1
+    ).astype(jnp.bfloat16)
+
+
+def depth_inputs(hidden, before, embed, gain):
+    looked = dot(jnp.where(chosen(before, embed.shape[0]), 1.0, 0.0).astype(jnp.bfloat16), embed)
+    inputs = jnp.concatenate([hidden] * CB, axis=0) + looked
+    scale = inverse_rms(inputs)
+    return inputs, scale, (inputs * scale * gain).astype(jnp.bfloat16)
+
+
+def depth_loss(head_in, ids, live, logit_weight):
+    logits = dot(head_in, logit_weight)
+    powers = jnp.exp(logits)
+    total = jnp.sum(powers, axis=-1, keepdims=True)
+    taken = chosen(ids, logits.shape[1])
+    row_loss = jnp.log(total) - jnp.sum(jnp.where(taken, logits, 0.0), axis=-1, keepdims=True)
+    frame_loss = sum(slab(row_loss, c) for c in range(CB)) * live
+    live_rows = jnp.concatenate([live] * CB, axis=0)
+    return frame_loss, (powers / total - jnp.where(taken, 1.0, 0.0)) * live_rows
+
+
+def whole_kernel(line, bucket, *refs):
+    (query, key, value, live, own_live, before, ids, places, gain_attn, gain_head) = refs[:10]
+    private, query_shard, key_shard, value_shard, out_shard, logit_shard, embed_shard = refs[10:17]
+    context, context_grad, losses = refs[17:20]
+    wholes = refs[20:25]
+    part_out, part_in, grads, loss_parts, loss_tiles = refs[25:30]
+    send_sem, recv_sem, local_sem, swap_send, swap_recv, tile_send, tile_recv = refs[30:]
+    proj_whole, embed_whole, qkv_whole, out_whole, logit_whole = wholes
+    count = 5
     seq, mp = lax.axis_index("seq"), lax.axis_index("mp")
+    seq_count = 2 * line
     zi, yi = seq // 2, seq % 2
     xi, ci = mp // 2, mp % 2
     z_peers = [lax.rem(zi + d, line) * 2 + yi for d in range(1, line)]
     y_peer = zi * 2 + (1 - yi)
     x_peer = (1 - xi) * 2 + ci
     c_peer = xi * 2 + (1 - ci)
+    diagonal = (1 - xi) * 2 + (1 - ci)
+    swap_peers = [c_peer, x_peer, diagonal]
+    shard_rows = [whole.shape[0] // seq_count for whole in wholes]
+    own = [
+        pl.ds(pl.multiple_of(seq * rows, rows), rows) for rows in shard_rows
+    ]
+    width = query_shard.shape[1]
+
+    locals_ = [
+        (private, proj_whole.at[own[0], :]),
+        (embed_shard, embed_whole.at[own[1], :]),
+        (query_shard, qkv_whole.at[own[2], 0:width]),
+        (key_shard, qkv_whole.at[own[2], width : 2 * width]),
+        (value_shard, qkv_whole.at[own[2], 2 * width : 3 * width]),
+        (out_shard, out_whole.at[own[3], :]),
+        (logit_shard, logit_whole.at[own[4], :]),
+    ]
+    local_copies = [
+        pltpu.make_async_copy(source, target, local_sem.at[at])
+        for at, (source, target) in enumerate(locals_)
+    ]
+    for copy in local_copies:
+        copy.start()
 
     barrier = pltpu.get_barrier_semaphore()
-    greeted = [(peer, mp) for peer in z_peers] + [(y_peer, mp), (seq, x_peer), (seq, c_peer)]
+    greeted = [(lax.rem(seq + d, seq_count), mp) for d in range(1, seq_count)]
+    greeted += [(seq, peer) for peer in swap_peers]
     for peer in greeted:
         pl.semaphore_signal(barrier, inc=1, device_id=peer, device_id_type=MESH)
     pl.semaphore_wait(barrier, len(greeted))
+    for copy in local_copies:
+        copy.wait()
 
     near = [lax.rem(zi + line - d, line) * 2 + yi for d in range(line)]
     far = [lax.rem(zi + line - d, line) * 2 + (1 - yi) for d in range(line)]
     others = near[1:] + far
 
     def rows_of(number, source, quarter):
-        rows = shards[number].shape[0]
+        rows = shard_rows[number]
         if number == 0:
             return pl.ds(pl.multiple_of(source * rows, rows), rows)
         part = rows // 4
@@ -119,27 +259,26 @@
 
     sends = []
 
-    def send(number, rows, slot, peer, src=None):
-        copy = pltpu.make_async_remote_copy(
-            src_ref=wholes[number].at[rows, :] if src is None else src,
-            dst_ref=wholes[number].at[rows, :],
-            send_sem=send_sem.at[number, slot],
-            recv_sem=recv_sem.at[number, slot],
+    def remote(source, target, leaving, landing, peer):
+        return pltpu.make_async_remote_copy(
+            src_ref=source,
+            dst_ref=target,
+            send_sem=leaving,
+            recv_sem=landing,
             device_id=peer,
             device_id_type=MESH,
         )
+
+    def send(number, rows, slot, peer):
+        here = wholes[number].at[rows, :]
+        copy = remote(here, here, send_sem.at[number, slot], recv_sem.at[number, slot], peer)
         copy.start()
         sends.append(copy)
 
     def arrived(number, rows, slot):
         here = wholes[number].at[rows, :]
-        pltpu.make_async_remote_copy(
-            src_ref=here,
-            dst_ref=here,
-            send_sem=send_sem.at[number, slot],
-            recv_sem=recv_sem.at[number, slot],
-            device_id=(seq, mp),
-            device_id_type=MESH,
+        remote(
+            here, here, send_sem.at[number, slot], recv_sem.at[number, slot], (seq, c_peer)
         ).wait_recv()
 
     z_at = 0
@@ -148,29 +287,13 @@
     c_at = x_at + 2 * line - 1
     xc_at = c_at + 2 * line - 1
 
-    own_copies = []
     for number in range(count):
-        rows = shards[number].shape[0]
-        if number == 0:
-            own = shards[number]
-        else:
-            part = rows // 4
-            own = shards[number].at[pl.ds(pl.multiple_of(mp * part, part), part), :]
         target = rows_of(number, seq, mp)
         for d in range(1, line):
-            send(number, target, z_at + d - 1, (z_peers[d - 1], mp), own)
-        send(number, target, y_at, (y_peer, mp), own)
-    for number in range(count):
-        rows = shards[number].shape[0]
-        copy = pltpu.make_async_copy(
-            shards[number],
-            wholes[number].at[pl.ds(pl.multiple_of(seq * rows, rows), rows), :],
-            local_sem.at[number],
-        )
-        copy.start()
-        own_copies.append(copy)
-
-    def share(number, rows, at):
+            send(number, target, z_at + d - 1, (z_peers[d - 1], mp))
+        send(number, target, y_at, (y_peer, mp))
+
+    def pass_on(number, rows, at):
         if number > 0:
             send(number, rows, x_at + at, (seq, x_peer))
             send(number, rows, c_at + at, (seq, c_peer))
@@ -180,11 +303,11 @@
             rows = rows_of(number, near[d], mp)
             arrived(number, rows, z_at + d - 1)
             send(number, rows, y_at + d, (y_peer, mp))
-            share(number, rows, d - 1)
+            pass_on(number, rows, d - 1)
         for d in range(line):
             rows = rows_of(number, far[d], mp)
             arrived(number, rows, y_at + d)
-            share(number, rows, line - 1 + d)
+            pass_on(number, rows, line - 1 + d)
 
     def cross_hops(number):
         for at, source in enumerate(others):
@@ -192,46 +315,226 @@
             arrived(number, rows, x_at + at)
             send(number, rows, xc_at + at, (seq, c_peer))
 
-    for number in range(count):
-        first_hops(number)
-        if number > 1:
-            cross_hops(number - 1)
-    cross_hops(count - 1)
-    diagonal = (1 - xi) * 2 + (1 - ci)
-    for number in range(1, count):
+    def finish(number):
         for at, source in enumerate(others):
             arrived(number, rows_of(number, source, c_peer), c_at + at)
             arrived(number, rows_of(number, source, diagonal), xc_at + at)
-    for copy in own_copies:
-        copy.wait()
+
+    for head in range(query.shape[1] // HEAD_T):
+        columns = slice(head * HEAD_T, (head + 1) * HEAD_T)
+        context[:, columns] = temporal_head(
+            query[:, columns], key[:, columns], value[:, columns], live[...]
+        )
+
+    first_hops(0)
+    share = part_in.shape[1]
+    partial = dot(context[...], proj_whole[...]).astype(jnp.bfloat16)
+    for part in range(CB):
+        part_out[part] = partial[part * share : (part + 1) * share]
+    for at, peer in enumerate(swap_peers):
+        copy = remote(
+            part_out.at[peer], part_in.at[at], swap_send.at[0, at], swap_recv.at[0, at], (seq, peer)
+        )
+        copy.start()
+        sends.append(copy)
+
+    first_hops(1)
+    first_hops(2)
+    cross_hops(1)
+    hidden = part_out[mp].astype(jnp.float32)
+    for at, peer in enumerate(swap_peers):
+        remote(
+            part_out.at[peer], part_in.at[at], swap_send.at[0, at], swap_recv.at[0, at], (seq, peer)
+        ).wait_recv()
+        hidden = hidden + part_in[at].astype(jnp.float32)
+    hidden = hidden.astype(jnp.bfloat16).astype(jnp.float32)
+    first_hops(3)
+    cross_hops(2)
+    finish(1)
+    inputs, scale, normed = depth_inputs(hidden, before[...], embed_whole[...], gain_attn[...])
+    first_hops(4)
+    cross_hops(3)
+    finish(2)
+    qkv = dot(normed, qkv_whole[...]).astype(jnp.bfloat16)
+    mixed, saved = depth_attention(qkv)
+    cross_hops(4)
+    finish(3)
+    residual = inputs + dot(mixed.astype(jnp.bfloat16), out_whole[...])
+    head_scale = inverse_rms(residual)
+    head_in = (residual * head_scale * gain_head[...]).astype(jnp.bfloat16)
+    finish(4)
+    frame_loss, logit_grad = depth_loss(head_in, ids[...], own_live[...], logit_whole[...])
+
+    spots = (seq_count, frame_loss.shape[0], loss_parts.shape[2])
+    lanes = lax.broadcasted_iota(jnp.int32, spots, 2)
+    spot = lax.broadcasted_iota(jnp.int32, spots, 0) * bucket + lanes
+    hit = jnp.logical_and(spot == places[...][None, :, :], lanes < bucket)
+    loss_parts[3] = jnp.sum(jnp.where(hit, frame_loss[None, :, :], 0.0), axis=1)
+    for at, peer in enumerate(swap_peers):
+        copy = remote(
+            loss_parts.at[3], loss_parts.at[at], swap_send.at[1, at], swap_recv.at[1, at], (seq, peer)
+        )
+        copy.start()
+        sends.append(copy)
+
+    head_grad = dot_turned(logit_grad.astype(jnp.bfloat16), logit_whole[...])
+    head_grad = head_grad.astype(jnp.bfloat16).astype(jnp.float32)
+    residual_grad = rms_back(residual, head_scale, gain_head[...], head_grad)
+    mixture_grad = dot_turned(residual_grad.astype(jnp.bfloat16), out_whole[...])
+    mixture_grad = mixture_grad.astype(jnp.bfloat16).astype(jnp.float32)
+    qkv_grad = depth_attention_back(mixture_grad, mixed, saved)
+    normed_grad = dot_turned(qkv_grad, qkv_whole[...]).astype(jnp.bfloat16).astype(jnp.float32)
+    inputs_grad = residual_grad + rms_back(inputs, scale, gain_attn[...], normed_grad)
+    grads[mp] = sum(slab(inputs_grad, c) for c in range(CB)).astype(jnp.bfloat16)
+    for at, peer in enumerate(swap_peers):
+        copy = remote(
+            grads.at[mp], grads.at[mp], swap_send.at[2, at], swap_recv.at[2, at], (seq, peer)
+        )
+        copy.start()
+        sends.append(copy)
+
+    for at, peer in enumerate(swap_peers):
+        remote(
+            loss_parts.at[3], loss_parts.at[at], swap_send.at[1, at], swap_recv.at[1, at], (seq, peer)
+        ).wait_recv()
+    loss_tiles[seq] = loss_parts[0] + loss_parts[1] + loss_parts[2] + loss_parts[3]
+    for d in range(1, seq_count):
+        copy = remote(
+            loss_tiles.at[seq],
+            loss_tiles.at[seq],
+            tile_send.at[d - 1],
+            tile_recv.at[d - 1],
+            (lax.rem(seq + d, seq_count), mp),
+        )
+        copy.start()
+        sends.append(copy)
+
+    for at, peer in enumerate(swap_peers):
+        remote(
+            grads.at[peer], grads.at[peer], swap_send.at[2, at], swap_recv.at[2, at], (seq, peer)
+        ).wait_recv()
+    rows = jnp.concatenate([grads[part] for part in range(CB)], axis=0)
+    context_grad[...] = dot_turned(rows, proj_whole[...]).astype(jnp.bfloat16)
+    for d in range(1, seq_count):
+        source = lax.rem(seq + seq_count - d, seq_count)
+        remote(
+            loss_tiles.at[source],
+            loss_tiles.at[source],
+            tile_send.at[d - 1],
+            tile_recv.at[d - 1],
+            (source, mp),
+        ).wait_recv()
+    losses[...] = loss_tiles[...]
     for copy in sends:
         copy.wait_send()
 
 
-def gather_all(private, shared):
-    seq_count = lax.axis_size("seq")
-    shards = (private,) + shared
-    small = private.shape[0] % 16 or any(part.shape[0] % 64 for part in shared)
-    if small or seq_count != 8 or lax.axis_size("mp") != 4:
-        return tuple(lax.all_gather(part, "seq", axis=0, tiled=True) for part in shards)
+def whole_step(
+    query_states,
+    key_states,
+    value_states,
+    lengths,
+    tokens,
+    assignment,
+    proj_weight,
+    query_weight,
+    key_weight,
+    value_weight,
+    out_weight,
+    logit_weight,
+    embedding,
+    gain_attn,
+    gain_head,
+):
+    seq_count, mp_count = lax.axis_size("seq"), lax.axis_size("mp")
+    seq_index, mp_index = lax.axis_index("seq"), lax.axis_index("mp")
+    frame_count, local_width = query_states.shape
+    share = frame_count // mp_count
+    slot_cap = 2 * frame_count
+    bucket = slot_cap // seq_count
+    model_width = proj_weight.shape[1]
+    first = mp_index * share
+    live = (jnp.arange(frame_count) < lengths[seq_index]).astype(jnp.float32)[:, None]
+    own_tokens = lax.dynamic_slice_in_dim(tokens, first, share).T
+    none = jnp.full((1, share), -1, jnp.int32)
+    before = jnp.concatenate([none, own_tokens[: CB - 1]], axis=0).reshape(-1, 1)
+    places = assignment // slot_cap * bucket + assignment % slot_cap - seq_index * bucket
     line = seq_count // 2
     slots = (line - 1) + line + 3 * (2 * line - 1)
-    count = len(shards)
-    return pl.pallas_call(
-        functools.partial(gather_kernel, line),
-        out_shape=tuple(
-            jax.ShapeDtypeStruct((part.shape[0] * seq_count, part.shape[1]), part.dtype)
-            for part in shards
+    vmem = pl.BlockSpec(memory_space=pltpu.VMEM)
+    shard = pl.BlockSpec(memory_space=pl.ANY)
+    depth_width = 3 * query_weight.shape[1]
+    context, context_grad, tiles = pl.pallas_call(
+        functools.partial(whole_kernel, line, bucket),
+        out_shape=(
+            jax.ShapeDtypeStruct((frame_count, local_width), jnp.bfloat16),
+            jax.ShapeDtypeStruct((frame_count, local_width), jnp.bfloat16),
+            jax.ShapeDtypeStruct((seq_count, seq_count, 128), jnp.float32),
         ),
-        in_specs=[pl.BlockSpec(memory_space=pl.ANY)] * count,
-        out_specs=tuple([pl.BlockSpec(memory_space=pl.ANY)] * count),
+        in_specs=[vmem] * 10 + [shard] * 7,
+        out_specs=(vmem, vmem, vmem),
         scratch_shapes=[
-            pltpu.SemaphoreType.DMA((count, slots)),
-            pltpu.SemaphoreType.DMA((count, slots)),
-            pltpu.SemaphoreType.DMA((count,)),
+            pltpu.VMEM((proj_weight.shape[0] * seq_count, model_width), jnp.bfloat16),
+            pltpu.VMEM((embedding.shape[0] * seq_count, model_width), jnp.bfloat16),
+            pltpu.VMEM((query_weight.shape[0] * seq_count, depth_width), jnp.bfloat16),
+            pltpu.VMEM((out_weight.shape[0] * seq_count, model_width), jnp.bfloat16),
+            pltpu.VMEM((logit_weight.shape[0] * seq_count, logit_weight.shape[1]), jnp.bfloat16),
+            pltpu.VMEM((mp_count, share, model_width), jnp.bfloat16),
+            pltpu.VMEM((mp_count - 1, share, model_width), jnp.bfloat16),
+            pltpu.VMEM((mp_count, share, model_width), jnp.bfloat16),
+            pltpu.VMEM((mp_count, seq_count, 128), jnp.float32),
+            pltpu.VMEM((seq_count, seq_count, 128), jnp.float32),
+            pltpu.SemaphoreType.DMA((5, slots)),
+            pltpu.SemaphoreType.DMA((5, slots)),
+            pltpu.SemaphoreType.DMA((7,)),
+            pltpu.SemaphoreType.DMA((3, mp_count - 1)),
+            pltpu.SemaphoreType.DMA((3, mp_count - 1)),
+            pltpu.SemaphoreType.DMA((seq_count - 1,)),
+            pltpu.SemaphoreType.DMA((seq_count - 1,)),
         ],
-        compiler_params=pltpu.CompilerParams(collective_id=0, has_side_effects=True),
-    )(*shards)
+        compiler_params=pltpu.CompilerParams(
+            collective_id=0, has_side_effects=True, vmem_limit_bytes=48 * 1024 * 1024
+        ),
+    )(
+        query_states,
+        key_states,
+        value_states,
+        live,
+        lax.dynamic_slice_in_dim(live, first, share),
+        before,
+        own_tokens.reshape(-1, 1),
+        lax.dynamic_slice_in_dim(places, first, share)[:, None],
+        gain_attn[None, :],
+        gain_head[None, :],
+        proj_weight,
+        query_weight,
+        key_weight,
+        value_weight,
+        out_weight,
+        logit_weight,
+        embedding,
+    )
+    sources = slot_cap // mp_count // bucket
+    mine = lax.dynamic_slice(
+        tiles, (mp_index * sources, seq_index, 0), (sources, 1, bucket)
+    )
+    return (context, context_grad, mine.reshape(-1))
+
+
+def fits(query_states, proj_weight, embedding, out_weight):
+    seq_count = lax.axis_size("seq")
+    return (
+        seq_count == 8
+        and lax.axis_size("mp") == 4
+        and query_states.shape[0] % 128 == 0
+        and proj_weight.shape[0] % 16 == 0
+        and embedding.shape[0] % 64 == 0
+        and out_weight.shape[0] % 64 == 0
+    )
+
+
+def gather_all(*shards):
+    return tuple(lax.all_gather(part, "seq", axis=0, tiled=True) for part in shards)
 
 
 def body(
@@ -251,7 +554,24 @@
     gain_attn,
     gain_head,
 ):
-    seq_count = lax.axis_size("seq")
+    if fits(query_states, proj_weight, embedding, out_weight):
+        return whole_step(
+            query_states,
+            key_states,
+            value_states,
+            lengths,
+            tokens,
+            assignment,
+            proj_weight,
+            query_weight,
+            key_weight,
+            value_weight,
+            out_weight,
+            logit_weight,
+            embedding,
+            gain_attn,
+            gain_head,
+        )
     seq_index = lax.axis_index("seq")
     frame_count = query_states.shape[0]
     local_width = query_states.shape[1]
@@ -279,12 +599,10 @@
     context = (mixture.reshape(frame_count, local_width) * live_mask[:, None]).astype(jnp.bfloat16)
     proj_quarter, embed_full, qkv_full, out_full, logit_full = gather_all(
         proj_weight,
-        (
-            embedding,
-            jnp.concatenate([query_weight, key_weight, value_weight], axis=1),
-            out_weight,
-            logit_weight,
-        ),
+        embedding,
+        jnp.concatenate([query_weight, key_weight, value_weight], axis=1),
+        out_weight,
+        logit_weight,
     )
     query_full, key_full, value_full = jnp.split(qkv_full, 3, axis=1)
     mp_count = lax.axis_size("mp")

time: 197 us -> 100 us (0.51)
  blocking collectives: 64.7 us -> 0 us
  matrix products: 23.2 us -> 0 us
  Pallas kernels: 71.3 us -> 84.7 us
  other arithmetic: 12.1 us -> 2.01 us
  local copies, waits for them, and re-layouts: 19 us -> 12.5 us
  starting transfers between devices: 3.4 us -> 0 us
    unnamed x1 -> x0, blocking collectives: 36.9 us -> none
    all_gather x2 -> x0, blocking collectives: 27.8 us -> none  [the longest x1 21.6 us: body(): frame_slot = lax.all_gather(assignment, 'seq', axis=0, tiled=True)]
    dot_general x20 -> x0, matrix products: 23.2 us -> none  [the longest x2 3.33 us: depth_losses(): jnp.dot(normed, value_weight, preferred_element_type=jnp.float32)]
    pallas_call x1, Pallas kernels: 71.3 us -> 84.7 us  [whole_step(): pl.pallas_call(functools.partial(whole_kernel, line, bucket), out_shape=(...]
    unnamed x79 -> x28, local copies, waits for them, and re-layouts: 2.94 us -> 10.1 us
    reduce_sum x8 -> x0, other arithmetic: 5.21 us -> none  [the longest x1 1.41 us: depth_losses(): inputs = hidden.astype(jnp.float32)[:, None, :] + looked]
    reshape x15 -> x3, local copies, waits for them, and re-layouts: 5.2 us -> 0.8 us  [the longest x1 0.59 us: whole_step(): return (context, context_grad, mine.reshape(-1))]
    gather x4 -> x0, local copies, waits for them, and re-layouts: 4.25 us -> none  [the longest x2 3.34 us: depth_losses(): jnp.take_along_axis(logits, token_ids.reshape(row_count, 1), axis=1)[:, 0]]
  transfers between devices with their start and end apart: 1 -> 0, of which waited for: 0 -> 0; matrix products, arithmetic and copies ran while one was open for 1% -> 0% of each run, Pallas kernels for 0% -> 0%
where the time goes in v2:
time: 100 us
  Pallas kernels  84.7 us (85%)
  local copies, waits for them, and re-layouts  12.5 us (12%)
  other arithmetic  2.01 us (2%)
    pallas_call x1, Pallas kernels, whole_step(): pl.pallas_call(functools.partial(whole_kernel, line, bucket), out_shape=(...  84.7 us
    unnamed x28, local copies, waits for them, and re-layouts  10.1 us

profile of v2, /device:TPU:0, one launch (start us, length us, event | category | flops | bytes accessed | tf_op | source)
XLA Modules:
  0.0 100.0 jit_solution(4609828905706284421)
XLA Ops:
  0.6 0.0 copy-start
  0.6 0.0 copy-start.1
  0.7 0.7 fusion.2
  1.4 0.1 dynamic-slice_bitcast_fusion.1
  1.5 1.2 %dynamic_slice.15 = s32[1]{0:T(128)} dynamic-slice(s32[8]{0:T(128)} %param.18, s32[]{:T(128)S(6)} %select_n.24), dynamic_slice_sizes={1} | dynamic-slice | bytes 12 | tf_op jit(solution)/shard_map/dynamic_slice | solution.py:457
  2.7 0.6 compare_convert_fusion
  3.3 0.1 dynamic-slice_bitcast_fusion.2
  3.4 0.0 copy-done
  3.4 0.1 dynamic-slice_bitcast_fusion
  3.5 0.1 copy.18.refs_4_
  3.6 0.1 copy.21.refs_7_
  3.7 0.1 reshape.29.refs_5_
  3.8 0.7 fusion.refs_3_
  4.5 0.0 copy-start.11
  4.5 0.0 copy-start.12
  4.5 0.1 reshape.30.refs_6_
  4.6 0.0 copy-done.1
  4.6 0.5 copy-done.11
  5.2 0.0 copy-done.12
  5.2 0.0 copy-start.2
  5.2 0.9 copy-done.2
  6.1 0.0 copy-start.3
  6.1 0.9 copy-done.3
  7.0 0.0 copy-start.4
  7.0 0.9 copy-done.4
  7.9 0.0 copy-start.5
  7.9 0.9 copy-done.5
  8.8 0.0 copy-start.6
  8.8 0.9 copy-done.6
  9.7 0.0 copy-start.7
  9.7 0.9 copy-done.7
  10.6 0.0 copy-start.8
  10.6 0.9 copy-done.8
  11.5 0.0 copy-start.9
  11.5 0.9 copy-done.9
  12.5 0.0 copy-start.10
  12.5 0.9 copy-done.10
  13.4 84.7 %shard_map.166 = (bf16[128,512]{1,0:T(8,128)(2,1)S(1)}, bf16[128,512]{1,0:T(8,128)(2,1)S(1)}, f32[8,8,128]{2,1,0:T(8,128)S(1)}) custom-call(bf16[128,512]{1,0:T(8,128)(2,1)S(1)} %copy-done.3, bf16[128,512]{1,0:T(8,128)(2,1)S(1)} %copy-done.4, bf16[128,512]{1,0:T(8,128)(2,1)S(1)} %copy-done.5, f32[128,1]{1,0:T(8,128)S(1)} %fusion.refs_3_, ...), custom_call_target="tpu_custom_call" | custom-call | tf_op jit(solution)/shard_map/pallas_call | solution.py:467
  98.1 0.6 reshape.28
  98.7 0.7 copy.24
  99.3 0.7 copy.25
  (2 shorter events, 0.0 us)
Async XLA Ops:
  0.6 2.8 %copy-start = (s32[128,4]{0,1:T(4,128)S(1)}, s32[128,4]{0,1:T(4,128)}, u32[]{:S(2)}) copy-start(s32[128,4]{0,1:T(4,128)} %param.19) | copy-start | bytes 6148
  0.6 4.0 %copy-start.1 = (bf16[128,1024]{1,0:T(8,128)(2,1)S(1)}, bf16[128,1024]{1,0:T(8,128)(2,1)}, u32[]{:S(2)}) copy-start(bf16[128,1024]{1,0:T(8,128)(2,1)} %refs_15_.1) | copy-start | bytes 786436
  4.5 0.7 copy-start.11
  4.5 0.7 copy-start.12
  5.2 0.9 copy-start.2
  6.1 0.9 copy-start.3
  7.0 0.9 copy-start.4
  7.9 0.9 copy-start.5
  8.8 0.9 copy-start.6
  9.7 0.9 copy-start.7
  10.6 0.9 copy-start.8
  11.5 0.9 copy-start.9
  12.5 0.9 copy-start.10

commit v3 on v2

--- a/solution.py
+++ b/solution.py
@@ -88,6 +88,8 @@
 MESH = pl.DeviceIdType.MESH
 
 
+ORDER = (1, 0, 2, 3, 4)
+AHEAD = 2
 PAIRS = [(c, k) for c in range(CB) for k in range(c + 1)]
 
 
@@ -197,12 +199,13 @@
 
 
 def whole_kernel(line, bucket, *refs):
-    (query, key, value, live, own_live, before, ids, places, gain_attn, gain_head) = refs[:10]
-    private, query_shard, key_shard, value_shard, out_shard, logit_shard, embed_shard = refs[10:17]
-    context, context_grad, losses = refs[17:20]
-    wholes = refs[20:25]
-    part_out, part_in, grads, loss_parts, loss_tiles = refs[25:30]
-    send_sem, recv_sem, local_sem, swap_send, swap_recv, tile_send, tile_recv = refs[30:]
+    lengths, tokens, assignment, gain_attn, gain_head = refs[:5]
+    query_states, key_states, value_states = refs[5:8]
+    private, query_shard, key_shard, value_shard, out_shard, logit_shard, embed_shard = refs[8:15]
+    context, context_grad, losses = refs[15:18]
+    wholes = refs[18:23]
+    part_out, part_in, grads, loss_parts, loss_tiles, query, key, value = refs[23:31]
+    send_sem, recv_sem, local_sem, swap_send, swap_recv, tile_send, tile_recv = refs[31:]
     proj_whole, embed_whole, qkv_whole, out_whole, logit_whole = wholes
     count = 5
     seq, mp = lax.axis_index("seq"), lax.axis_index("mp")
@@ -229,6 +232,9 @@
         (value_shard, qkv_whole.at[own[2], 2 * width : 3 * width]),
         (out_shard, out_whole.at[own[3], :]),
         (logit_shard, logit_whole.at[own[4], :]),
+        (query_states, query),
+        (key_states, key),
+        (value_states, value),
     ]
     local_copies = [
         pltpu.make_async_copy(source, target, local_sem.at[at])
@@ -243,7 +249,7 @@
     for peer in greeted:
         pl.semaphore_signal(barrier, inc=1, device_id=peer, device_id_type=MESH)
     pl.semaphore_wait(barrier, len(greeted))
-    for copy in local_copies:
+    for copy in local_copies[:7]:
         copy.wait()
 
     near = [lax.rem(zi + line - d, line) * 2 + yi for d in range(line)]
@@ -287,11 +293,14 @@
     c_at = x_at + 2 * line - 1
     xc_at = c_at + 2 * line - 1
 
-    for number in range(count):
+    def own_sends(number):
         target = rows_of(number, seq, mp)
+        send(number, target, y_at, (y_peer, mp))
         for d in range(1, line):
             send(number, target, z_at + d - 1, (z_peers[d - 1], mp))
-        send(number, target, y_at, (y_peer, mp))
+
+    for number in ORDER[:AHEAD]:
+        own_sends(number)
 
     def pass_on(number, rows, at):
         if number > 0:
@@ -299,12 +308,15 @@
             send(number, rows, c_at + at, (seq, c_peer))
 
     def first_hops(number):
-        for d in range(1, line):
-            rows = rows_of(number, near[d], mp)
-            arrived(number, rows, z_at + d - 1)
-            send(number, rows, y_at + d, (y_peer, mp))
-            pass_on(number, rows, d - 1)
+        later = ORDER.index(number) + AHEAD
+        if later < count:
+            own_sends(ORDER[later])
         for d in range(line):
+            if d > 0:
+                rows = rows_of(number, near[d], mp)
+                arrived(number, rows, z_at + d - 1)
+                send(number, rows, y_at + d, (y_peer, mp))
+                pass_on(number, rows, d - 1)
             rows = rows_of(number, far[d], mp)
             arrived(number, rows, y_at + d)
             pass_on(number, rows, line - 1 + d)
@@ -320,13 +332,21 @@
             arrived(number, rows_of(number, source, c_peer), c_at + at)
             arrived(number, rows_of(number, source, diagonal), xc_at + at)
 
+    for copy in local_copies[7:]:
+        copy.wait()
+    frames = query.shape[0]
+    length = lengths[seq]
+    live = jnp.where(
+        lax.broadcasted_iota(jnp.int32, (frames, 1), 0) < length, 1.0, 0.0
+    )
     for head in range(query.shape[1] // HEAD_T):
         columns = slice(head * HEAD_T, (head + 1) * HEAD_T)
         context[:, columns] = temporal_head(
-            query[:, columns], key[:, columns], value[:, columns], live[...]
+            query[:, columns], key[:, columns], value[:, columns], live
         )
 
-    first_hops(0)
+    for number in ORDER[:2]:
+        first_hops(number)
     share = part_in.shape[1]
     partial = dot(context[...], proj_whole[...]).astype(jnp.bfloat16)
     for part in range(CB):
@@ -338,9 +358,19 @@
         copy.start()
         sends.append(copy)
 
-    first_hops(1)
+    cross_hops(1)
     first_hops(2)
-    cross_hops(1)
+    first = pl.multiple_of(mp * share, share)
+    own_tokens = tokens[pl.ds(first, share), :]
+    columns = [own_tokens[:, c : c + 1] for c in range(CB)]
+    ids = jnp.concatenate(columns, axis=0)
+    before = jnp.concatenate([jnp.full((share, 1), -1, jnp.int32)] + columns[:-1], axis=0)
+    frame = first + lax.broadcasted_iota(jnp.int32, (share, 1), 0)
+    own_live = jnp.where(frame < length, 1.0, 0.0)
+    own_frame = lax.broadcasted_iota(jnp.int32, (share, frames), 1) == frame
+    slot = jnp.sum(jnp.where(own_frame, assignment[...], 0), axis=1, keepdims=True)
+    slot_cap = bucket * seq_count
+    places = slot // slot_cap * bucket + slot % slot_cap - seq * bucket
     hidden = part_out[mp].astype(jnp.float32)
     for at, peer in enumerate(swap_peers):
         remote(
@@ -351,7 +381,7 @@
     first_hops(3)
     cross_hops(2)
     finish(1)
-    inputs, scale, normed = depth_inputs(hidden, before[...], embed_whole[...], gain_attn[...])
+    inputs, scale, normed = depth_inputs(hidden, before, embed_whole[...], gain_attn[...])
     first_hops(4)
     cross_hops(3)
     finish(2)
@@ -363,12 +393,12 @@
     head_scale = inverse_rms(residual)
     head_in = (residual * head_scale * gain_head[...]).astype(jnp.bfloat16)
     finish(4)
-    frame_loss, logit_grad = depth_loss(head_in, ids[...], own_live[...], logit_whole[...])
+    frame_loss, logit_grad = depth_loss(head_in, ids, own_live, logit_whole[...])
 
     spots = (seq_count, frame_loss.shape[0], loss_parts.shape[2])
     lanes = lax.broadcasted_iota(jnp.int32, spots, 2)
     spot = lax.broadcasted_iota(jnp.int32, spots, 0) * bucket + lanes
-    hit = jnp.logical_and(spot == places[...][None, :, :], lanes < bucket)
+    hit = jnp.logical_and(spot == places[None, :, :], lanes < bucket)
     loss_parts[3] = jnp.sum(jnp.where(hit, frame_loss[None, :, :], 0.0), axis=1)
     for at, peer in enumerate(swap_peers):
         copy = remote(
@@ -453,12 +483,6 @@
     slot_cap = 2 * frame_count
     bucket = slot_cap // seq_count
     model_width = proj_weight.shape[1]
-    first = mp_index * share
-    live = (jnp.arange(frame_count) < lengths[seq_index]).astype(jnp.float32)[:, None]
-    own_tokens = lax.dynamic_slice_in_dim(tokens, first, share).T
-    none = jnp.full((1, share), -1, jnp.int32)
-    before = jnp.concatenate([none, own_tokens[: CB - 1]], axis=0).reshape(-1, 1)
-    places = assignment // slot_cap * bucket + assignment % slot_cap - seq_index * bucket
     line = seq_count // 2
     slots = (line - 1) + line + 3 * (2 * line - 1)
     vmem = pl.BlockSpec(memory_space=pltpu.VMEM)
@@ -471,7 +495,7 @@
             jax.ShapeDtypeStruct((frame_count, local_width), jnp.bfloat16),
             jax.ShapeDtypeStruct((seq_count, seq_count, 128), jnp.float32),
         ),
-        in_specs=[vmem] * 10 + [shard] * 7,
+        in_specs=[pl.BlockSpec(memory_space=pltpu.SMEM)] + [vmem] * 4 + [shard] * 10,
         out_specs=(vmem, vmem, vmem),
         scratch_shapes=[
             pltpu.VMEM((proj_weight.shape[0] * seq_count, model_width), jnp.bfloat16),
@@ -484,28 +508,29 @@
             pltpu.VMEM((mp_count, share, model_width), jnp.bfloat16),
             pltpu.VMEM((mp_count, seq_count, 128), jnp.float32),
             pltpu.VMEM((seq_count, seq_count, 128), jnp.float32),
+            pltpu.VMEM((frame_count, local_width), jnp.bfloat16),
+            pltpu.VMEM((frame_count, local_width), jnp.bfloat16),
+            pltpu.VMEM((frame_count, local_width), jnp.bfloat16),
             pltpu.SemaphoreType.DMA((5, slots)),
             pltpu.SemaphoreType.DMA((5, slots)),
-            pltpu.SemaphoreType.DMA((7,)),
+            pltpu.SemaphoreType.DMA((10,)),
             pltpu.SemaphoreType.DMA((3, mp_count - 1)),
             pltpu.SemaphoreType.DMA((3, mp_count - 1)),
             pltpu.SemaphoreType.DMA((seq_count - 1,)),
             pltpu.SemaphoreType.DMA((seq_count - 1,)),
         ],
         compiler_params=pltpu.CompilerParams(
-            collective_id=0, has_side_effects=True, vmem_limit_bytes=48 * 1024 * 1024
+            collective_id=0, has_side_effects=True, vmem_limit_bytes=60 * 1024 * 1024
         ),
     )(
+        lengths,
+        tokens,
+        assignment[None, :],
+        gain_attn[None, :],
+        gain_head[None, :],
         query_states,
         key_states,
         value_states,
-        live,
-        lax.dynamic_slice_in_dim(live, first, share),
-        before,
-        own_tokens.reshape(-1, 1),
-        lax.dynamic_slice_in_dim(places, first, share)[:, None],
-        gain_attn[None, :],
-        gain_head[None, :],
         proj_weight,
         query_weight,
         key_weight,

time: 100 us -> 94.4 us (0.944)
  local copies, waits for them, and re-layouts: 12.5 us -> 4.99 us
  Pallas kernels: 84.7 us -> 88.5 us
  other arithmetic: 2.01 us -> 0 us
    unnamed x28 -> x7, local copies, waits for them, and re-layouts: 10.1 us -> 3.68 us
    pallas_call x1, Pallas kernels: 84.7 us -> 88.5 us  [whole_step(): pl.pallas_call(functools.partial(whole_kernel, line, bucket), out_shape=(...]
    dynamic_slice x3 -> x0, local copies, waits for them, and re-layouts: 1.4 us -> none  [the longest x1 1.24 us: whole_step(): lengths[seq_index]]
    convert_element_type x2 -> x0, other arithmetic: 1.3 us -> none  [whole_step(): (jnp.arange(frame_count) < lengths[seq_index]).astype(jnp.float32)[:, None]]
where the time goes in v3:
time: 94.4 us; the launch traced here: 94.1 us
  Pallas kernels  88.5 us (94%)
  local copies, waits for them, and re-layouts  4.99 us (5%)
    pallas_call x1, Pallas kernels, whole_step(): pl.pallas_call(functools.partial(whole_kernel, line, bucket), out_shape=(...  88.5 us
    unnamed x7, local copies, waits for them, and re-layouts  3.68 us

profile of v3, /device:TPU:0, one launch (start us, length us, event | category | flops | bytes accessed | tf_op | source)
XLA Modules:
  0.0 94.1 jit_solution(15673610521945860257)
XLA Ops:
  0.6 0.0 copy-start.1
  0.6 0.7 copy-done.1
  1.3 0.7 copy.18.refs_1_
  2.1 88.5 %shard_map.166 = (bf16[128,512]{1,0:T(8,128)(2,1)}, bf16[128,512]{1,0:T(8,128)(2,1)}, f32[8,8,128]{2,1,0:T(8,128)}) custom-call(s32[8]{0:T(128)} %refs_0_.1, s32[128,4]{1,0:T(8,128)} %copy.18.refs_1_, s32[1,128]{1,0:T(1,128)} %bitcast.5, f32[1,1024]{1,0:T(1,128)} %bitcast.3, f32[1,1024]{1,0:T(1,128)} %bitcast.4, bf16[128,512]{1,0:T(8,128)(2,1)} %refs_5_.1, ...), custom_call_target="tpu_custom_call" | custom-call | tf_op jit(solution)/shard_map/pallas_call | solution.py:491
  90.6 0.7 dynamic-slice_reduce_fusion
  91.3 0.6 reshape.9
  91.9 0.0 copy-start
  91.9 1.6 %copy.21 = bf16[128,512]{1,0:T(8,128)(2,1)} copy(bf16[128,512]{1,0:T(8,128)(2,1)} %get-tuple-element.12) | data formatting | bytes 262144
  93.5 0.0 copy-done
  93.5 0.7 copy.22
Async XLA Ops:
  0.6 0.7 copy-start.1
  91.9 1.6 %copy-start = (bf16[128,512]{1,0:T(8,128)(2,1)S(1)}, bf16[128,512]{1,0:T(8,128)(2,1)}, u32[]{:S(2)}) copy-start(bf16[128,512]{1,0:T(8,128)(2,1)} %get-tuple-element.13) | copy-start | bytes 393220
